TPU v7x, 32 devices: a whole 2x2x4 slice. The times are simulated.
32 devices in a mesh: dp: 8 (over y, x, core), tensor: 4 (over z).
Axes of the slice: x: 2, y: 2, z: 4, core: 2. Of those that a mesh axis runs over, the one named last changes fastest.
Arguments:
- tokens: bfloat16 [8192, 1024], P('dp'), may hold values from -6 to 6
- memory: bfloat16 [8, 1024, 1024], P('dp'), may hold values from -6 to 6
- segments: int32 [8, 2048], P('dp'), may hold values from 0 to 3, never falling along the last dimension, each value on 1 to 1024 neighbouring positions
- value_routes: int32 [8, 2048, 4, 2], P('dp', None, 'tensor'), may hold values from 0 to 4, all different within a row
- output_routes: int32 [8192, 4, 2], P('dp', 'tensor'), may hold values from 0 to 4, all different within a row
- first_gain: float32 [1024], replicated, may hold values from 0.5 to 1.5
- first_bias: float32 [1024], replicated, may hold values from -4 to 4
- second_gain: float32 [1024], replicated, may hold values from 0.5 to 1.5
- second_bias: float32 [1024], replicated, may hold values from -4 to 4
- query_head_weight: bfloat16 [4, 1024, 112], P('tensor'), may hold values from -0.1875 to 0.1875
- key_weight: bfloat16 [4, 1024, 112], P('tensor'), may hold values from -0.1875 to 0.1875
- position_weight: bfloat16 [4, 1024, 112], P('tensor'), may hold values from -0.1875 to 0.1875
- value_weight: bfloat16 [4, 1024, 560], P('tensor'), may hold values from -0.1875 to 0.1875
- value_select: bfloat16 [4, 1024, 5], P('tensor'), may hold values from -0.375 to 0.375
- output_expert_selector: bfloat16 [4, 1024, 5], P('tensor'), may hold values from -0.375 to 0.375
- output_expert_weight: bfloat16 [4, 560, 1024], P('tensor'), may hold values from -3 to 3
- content_bias: float32 [4, 112], P('tensor'), may hold values from -6 to 6
- position_bias: float32 [4, 112], P('tensor'), may hold values from -6 to 6
- up_projection_weight: bfloat16 [1024, 4096], P(None, 'tensor'), may hold values from -0.1875 to 0.1875
- down_projection_weight: bfloat16 [4096, 1024], P('tensor'), may hold values from -0.125 to 0.125
- cotangent: bfloat16 [8192, 1024], P(('dp', 'tensor')), may hold values from -6 to 6
Outputs:
- result: bfloat16 [8192, 1024], P(('dp', 'tensor'))
- tokens_gradient: float32 [8192, 1024], P(('dp', 'tensor'))
- first_gain_gradient: float32 [1024], replicated
- first_bias_gradient: float32 [1024], replicated
- second_gain_gradient: float32 [1024], replicated
- second_bias_gradient: float32 [1024], replicated
- query_weight_gradient: float32 [4, 1024, 112], P('tensor', 'dp')
- key_weight_gradient: float32 [4, 1024, 112], P('tensor', 'dp')
- position_weight_gradient: float32 [4, 1024, 112], P('tensor', 'dp')
- value_weight_gradient: float32 [4, 1024, 560], P('tensor', 'dp')
- value_select_gradient: float32 [4, 1024, 5], P('tensor', 'dp')
- output_select_gradient: float32 [4, 1024, 5], P('tensor', 'dp')
- output_weight_gradient: float32 [4, 560, 1024], P('tensor', None, 'dp')
- content_bias_gradient: float32 [4, 112], replicated
- position_bias_gradient: float32 [4, 112], replicated
- up_weight_gradient: float32 [1024, 4096], P('dp', 'tensor')
- down_weight_gradient: float32 [4096, 1024], P('tensor', 'dp')
Inputs may be any that keep to these rules, and one draw needn't show every extreme that they name: `value_routes`: each row names 2 different value experts of its head. `output_routes`: each row names 2 different output experts of its head. `segments`: numbers never fall along a row.
All inputs are finite; a program needn't handle non-finite values.
Results may differ from a plain program's by a relative error of at most 0.023.
Values may be sent and summed in bfloat16 or wider, within the bound.
No kernel may reach another device: no remote copies, remote signals or barrier semaphores. Data moves between devices by JAX's collectives and lax.ppermute only.
A program may use at most 192 MiB of HBM per device.

v0:
```python
import functools
import math

import jax
import jax.numpy as jnp
from jax import lax
from jax.experimental import pallas as pl
from jax.experimental.pallas import tpu as pltpu
from jax.sharding import PartitionSpec as P

EPSILON = 1e-05
ROOT_HALF = 0.7071067811865476
INVERSE_ROOT_TAU = 0.3989422804014327
ROWS = 256
GROUP = 8
MIB = 1024 * 1024
BF16 = jnp.bfloat16
F32 = jnp.float32


def mm(left, right):
    return jnp.dot(left, right, preferred_element_type=F32)


def mm_nt(left, right):
    return lax.dot_general(left, right, (((1,), (1,)), ((), ())), preferred_element_type=F32)


def mm_tn(left, right):
    return lax.dot_general(left, right, (((0,), (0,)), ((), ())), preferred_element_type=F32)


def norm_parts(values):
    center = values - jnp.mean(values, axis=-1, keepdims=True)
    inv_std = lax.rsqrt(jnp.mean(center * center, axis=-1, keepdims=True) + EPSILON)
    return center * inv_std, inv_std


def norm_back(upstream, normal, inv_std, gain):
    scaled = upstream * gain
    return inv_std * (
        scaled
        - jnp.mean(scaled, axis=-1, keepdims=True)
        - normal * jnp.mean(scaled * normal, axis=-1, keepdims=True)
    )


def params():
    return pltpu.CompilerParams(vmem_limit_bytes=63 * MIB)


def cost(microseconds):
    return pl.CostEstimate(
        flops=int(microseconds * 1.15e9), bytes_accessed=0, transcendentals=0
    )


def struct(shape, dtype):
    return jax.ShapeDtypeStruct(shape, dtype)


def whole(*shape):
    return pl.BlockSpec(shape, lambda *_: (0,) * len(shape))

LANES = 128


def lane_of(rows):
    return lax.broadcasted_iota(jnp.int32, (rows, LANES), 1)


def picked(routes, head_dim):
    rows = routes.shape[1]
    routes = jnp.concatenate([routes, jnp.zeros((6, rows), jnp.int32)], axis=0).astype(F32).T
    lane = (lane_of(rows) - head_dim).astype(F32)
    return (lane == routes[:, 0:1]) | (lane == routes[:, 1:2])


def after(array, *deps, span=0):
    def body(*refs):
        del refs

    spec = pl.BlockSpec(memory_space=pl.ANY)
    return pl.pallas_call(
        body,
        in_specs=[spec] * (1 + len(deps)),
        out_specs=spec,
        out_shape=struct(array.shape, array.dtype),
        input_output_aliases={0: 0},
        cost_estimate=cost(span),
        name="after",
    )(array, *deps)


def together(*arrays, span=0):
    def body(*refs):
        del refs

    spec = pl.BlockSpec(memory_space=pl.ANY)
    return pl.pallas_call(
        body,
        in_specs=[spec] * len(arrays),
        out_specs=[spec] * len(arrays),
        out_shape=[struct(a.shape, a.dtype) for a in arrays],
        input_output_aliases={i: i for i in range(len(arrays))},
        cost_estimate=cost(span),
        name="together",
    )(*arrays)


def pile(*arrays):
    def body(*refs):
        for i, ref in enumerate(refs[:-1]):
            refs[-1][i] = ref[...]

    shape = arrays[0].shape
    return pl.pallas_call(
        body,
        in_specs=[whole(*shape)] * len(arrays),
        out_specs=whole(len(arrays), *shape),
        out_shape=struct((len(arrays),) + shape, arrays[0].dtype),
        grid=(1,),
        compiler_params=params(),
        cost_estimate=cost(2),
        name="pile",
    )(*arrays)


def project_kernel(
    experts,
    head_dim,
    mem_steps,
    scale,
    mem_ref,
    tok_ref,
    gain_ref,
    bias_ref,
    key_w_ref,
    vsel_ref,
    value_w_ref,
    query_w_ref,
    osel_ref,
    vroute_ref,
    oroute_ref,
    cb_ref,
    pb_ref,
    w_out_ref,
    normed_ref,
    key_ref,
    val_ref,
    every_ref,
    vgate_ref,
    qc_ref,
    qp_ref,
    ogate_ref,
    w_ref,
):
    step = pl.program_id(0)
    query = (1 + experts) * LANES

    @pl.when(step == 0)
    def _():
        w_ref[...] = jnp.zeros_like(w_ref)
        w_ref[:head_dim, :] = key_w_ref[...]
        w_ref[head_dim : head_dim + experts, :] = vsel_ref[...]
        for e in range(experts):
            w_ref[(1 + e) * LANES : (1 + e) * LANES + head_dim, :] = value_w_ref[
                e * head_dim : (e + 1) * head_dim, :
            ]
        w_ref[query : query + head_dim, :] = query_w_ref[...]
        w_ref[query + head_dim : query + head_dim + experts, :] = osel_ref[...]

    size = w_out_ref.shape[0]
    w_out_ref[...] = w_ref[pl.ds(pl.multiple_of(step * size, size), size), :]

    def rows_part():
        blocks = [slice(i * ROWS, (i + 1) * ROWS) for i in range(tok_ref.shape[0] // ROWS)]
        normed, outs = [], []
        for rows in blocks:
            block = jnp.where(step < mem_steps, mem_ref[rows, :], tok_ref[rows, :])
            normal, _ = norm_parts(block.astype(F32))
            normed.append((normal * gain_ref[...] + bias_ref[...]).astype(BF16))
            outs.append(mm_nt(normed[-1], w_ref[: query + LANES, :]))
        lane = lane_of(ROWS)
        real = lane < head_dim
        for rows, norm, out in zip(blocks, normed, outs):
            normed_ref[rows, :] = norm
            first = out[:, :LANES]
            key_ref[rows, :] = jnp.where(real, first, 0.0).astype(BF16)
            every_ref[rows, :] = out[:, LANES:query].astype(BF16)
            gate = jnp.where(picked(vroute_ref[:, rows], head_dim), jax.nn.sigmoid(first), 0.0)
            vgate_ref[rows, :] = gate
            value = jnp.zeros((ROWS, LANES), F32)
            for e in range(experts):
                value = value + gate[:, head_dim + e : head_dim + e + 1] * (
                    out[:, (1 + e) * LANES : (2 + e) * LANES]
                )
            val_ref[rows, :] = value.astype(BF16)
            q = out[:, query:]
            qc_ref[rows, :] = jnp.where(real, (q + cb_ref[...]) * scale, 0.0).astype(BF16)
            qp_ref[rows, :] = jnp.where(real, (q + pb_ref[...]) * scale, 0.0).astype(BF16)
            ogate_ref[rows, :] = jnp.where(
                picked(oroute_ref[:, rows], head_dim), jax.nn.sigmoid(q), 0.0
            )

    rows_part()


def project(memory, tokens, gain, bias, weights, vroutes, oroutes, cb, pb, experts, head_dim):
    mem, width = memory.shape
    toks = tokens.shape[0]
    big = 2 * ROWS
    mem_steps, tok_steps = mem // big, toks // big
    steps = mem_steps + tok_steps
    keys = mem + toks
    cols = width
    mem_row = lambda i: (jnp.minimum(i, mem_steps - 1), 0)
    tok_row = lambda i: (jnp.maximum(i - mem_steps, 0), 0)
    row = lambda i: (i, 0)
    return pl.pallas_call(
        functools.partial(project_kernel, experts, head_dim, mem_steps, head_dim ** (-0.5)),
        grid=(steps,),
        in_specs=[
            pl.BlockSpec((big, width), mem_row),
            pl.BlockSpec((big, width), tok_row),
            whole(1, width),
            whole(1, width),
        ]
        + [whole(*w.shape) for w in weights]
        + [
            pl.BlockSpec((vroutes.shape[0], big), lambda i: (0, i)),
            pl.BlockSpec((oroutes.shape[0], big), lambda i: (0, jnp.maximum(i - mem_steps, 0))),
            whole(1, LANES),
            whole(1, LANES),
        ],
        out_specs=[
            pl.BlockSpec((cols // steps, width), row),
            pl.BlockSpec((big, width), row),
            pl.BlockSpec((big, LANES), row),
            pl.BlockSpec((big, LANES), row),
            pl.BlockSpec((big, experts * LANES), row),
            pl.BlockSpec((big, LANES), row),
            pl.BlockSpec((big, LANES), tok_row),
            pl.BlockSpec((big, LANES), tok_row),
            pl.BlockSpec((big, LANES), tok_row),
        ],
        out_shape=[
            struct((cols, width), BF16),
            struct((keys, width), BF16),
            struct((keys, LANES), BF16),
            struct((keys, LANES), BF16),
            struct((keys, experts * LANES), BF16),
            struct((keys, LANES), F32),
            struct((toks, LANES), BF16),
            struct((toks, LANES), BF16),
            struct((toks, LANES), F32),
        ],
        scratch_shapes=[pltpu.VMEM((cols, width), BF16)],
        compiler_params=params(),
        cost_estimate=cost(12),
        name="project",
    )(memory, tokens, gain, bias, *weights, vroutes, oroutes, cb, pb)


def attend_kernel(
    span,
    head_dim,
    count,
    z_ref,
    qc_ref,
    qp_ref,
    key_ref,
    val_ref,
    rel_ref,
    segk_ref,
    segq_ref,
    ogate_ref,
    heads_ref,
    probs_ref,
    *pack_refs,
):
    step = pl.program_id(0)
    wide = span + ROWS
    column = lax.broadcasted_iota(jnp.int32, (ROWS, ROWS), 1)
    causal = column <= lax.broadcasted_iota(jnp.int32, (ROWS, ROWS), 0)
    for b in range(count):
        rows = slice(b * ROWS, (b + 1) * ROWS)
        window = pl.ds((step * count + b) * ROWS, wide)
        content = mm_nt(qc_ref[rows, :], key_ref[window, :])
        reverse = mm_nt(qp_ref[rows, :], rel_ref[...])
        reverse = jnp.concatenate([reverse, jnp.zeros((ROWS, ROWS), F32)], axis=1)
        scores = content + pltpu.roll(reverse, 1, 1, stride=1, stride_axis=0)
        same = segk_ref[b] == segq_ref[rows, :]
        allowed = jnp.concatenate([same[:, :span], same[:, span:] & causal], axis=1)
        scores = jnp.where(allowed, scores, -1e30)
        expo = jnp.exp(scores - jnp.max(scores, axis=1, keepdims=True))
        probs = (expo * (1.0 / jnp.sum(expo, axis=1, keepdims=True))).astype(BF16)
        probs_ref[rows, :] = probs
        heads = mm(probs, val_ref[window, :])
        heads_ref[rows, :] = heads
        packed = jnp.where(lane_of(ROWS) < head_dim, heads, ogate_ref[rows, :]).astype(BF16)
        slot = (step * count + b) ^ z_ref[0]
        for side, pack_ref in enumerate(pack_refs):

            @pl.when(slot // 2 == side)
            def _():
                pack_ref[slot % 2] = packed


def attend(rank, qc, qp, key_vecs, value_vecs, rel_reverse, seg_keys, seg_query, ogate, head_dim):
    toks = qc.shape[0]
    keys = key_vecs.shape[0]
    span = rel_reverse.shape[0]
    steps = toks // ROWS
    count = 1
    big = count * ROWS
    wide = span + ROWS
    row = lambda i, z: (i, 0)
    return pl.pallas_call(
        functools.partial(attend_kernel, span, head_dim, count),
        grid_spec=pltpu.PrefetchScalarGridSpec(
            num_scalar_prefetch=1,
            grid=(steps // count,),
            in_specs=[
                pl.BlockSpec((big, LANES), row),
                pl.BlockSpec((big, LANES), row),
                whole(keys, LANES),
                whole(keys, LANES),
                whole(span, LANES),
                pl.BlockSpec((count, 1, wide), lambda i, z: (i, 0, 0)),
                pl.BlockSpec((big, 1), row),
                pl.BlockSpec((big, LANES), row),
            ],
            out_specs=[
                pl.BlockSpec((big, LANES), row),
                pl.BlockSpec((big, wide), row),
            ]
            + [whole(2, ROWS, LANES)] * (steps // 2),
        ),
        out_shape=[struct((toks, LANES), F32), struct((toks, wide), BF16)]
        + [struct((2, ROWS, LANES), BF16)] * (steps // 2),
        compiler_params=params(),
        cost_estimate=cost(8),
        name="attend",
    )(rank, qc, qp, key_vecs, value_vecs, rel_reverse, seg_keys, seg_query, ogate)


def attend_back_kernel(
    span,
    experts,
    head_dim,
    parts,
    z_ref,
    qc_ref,
    qp_ref,
    key_ref,
    val_ref,
    rel_ref,
    probs_ref,
    heads_ref,
    ogate_ref,
    every_ref,
    vgate_ref,
    *refs,
):
    back_refs, refs = refs[: parts // 2], refs[parts // 2 :]
    key_grad_ref, value_grad_ref, query_grad_ref, rel_grad_ref, bias_ref = refs[:5]
    pack_refs, refs = refs[5 : 5 + parts // 2], refs[5 + parts // 2 :]
    keys_scr, values_scr, rel_scr, query_scr, back_scr = refs
    step = pl.program_id(0)
    steps = pl.num_programs(0)
    wide = span + ROWS
    mem = keys_scr.shape[0] - steps * ROWS
    scale = head_dim ** (-0.5)
    real = lane_of(ROWS) < head_dim

    @pl.when(step == 0)
    def _():
        keys_scr[...] = jnp.zeros_like(keys_scr)
        values_scr[...] = jnp.zeros_like(values_scr)
        rel_scr[...] = jnp.zeros_like(rel_scr)
        bias_ref[...] = jnp.zeros_like(bias_ref)

    slot = step ^ z_ref[0]
    for side, back_ref in enumerate(back_refs):

        @pl.when(slot // 2 == side)
        def _():
            back_scr[...] = back_ref[slot % 2]

    window = pl.ds(step * ROWS, wide)
    keys = key_ref[window, :]
    vals = val_ref[window, :]
    back = back_scr[...].astype(F32)
    out_grad = jnp.where(real, back, 0.0)
    delta = jnp.sum(out_grad * heads_ref[...], axis=1, keepdims=True)
    out_grad = out_grad.astype(BF16)
    probs = probs_ref[...]
    probs_grad = mm_nt(out_grad, vals)
    score_grad = (probs.astype(F32) * (probs_grad - delta)).astype(BF16)
    content_grad = mm(score_grad, keys).astype(BF16).astype(F32) * scale
    keys_scr[window, :] += mm_tn(score_grad, qc_ref[...])
    values_scr[window, :] += mm_tn(probs, out_grad)
    flip = (
        lax.broadcasted_iota(jnp.int32, (ROWS, ROWS), 0)
        + lax.broadcasted_iota(jnp.int32, (ROWS, ROWS), 1)
        == ROWS - 1
    ).astype(BF16)
    turned = mm(flip, score_grad)
    turned = pltpu.roll(turned, span, 1, stride=1, stride_axis=0)[:, :span].astype(BF16)
    place_grad = mm(turned, rel_ref[...]).astype(BF16)
    position_grad = mm(flip, place_grad) * scale
    rel_scr[...] += mm_tn(turned, mm(flip, qp_ref[...]).astype(BF16))
    bias_ref[0:1, :] += jnp.sum(content_grad, axis=0, keepdims=True)
    bias_ref[1:2, :] += jnp.sum(position_grad, axis=0, keepdims=True)
    gate = ogate_ref[...]
    query_grad = jnp.where(real, content_grad + position_grad, back * gate * (1.0 - gate))
    query_grad = query_grad.astype(BF16)
    query_grad_ref[...] = query_grad
    query_scr[pl.ds(step * ROWS, ROWS), :] = query_grad

    @pl.when(step == steps - 1)
    def _():
        rel_grad_ref[...] = rel_scr[...].astype(BF16)

        @pl.loop(0, (mem + steps * ROWS) // ROWS)
        def _(block):
            rows = pl.ds(block * ROWS, ROWS)
            value_grad = values_scr[rows, :]
            gates = vgate_ref[rows, :]
            value_grad_ref[rows, :] = value_grad
            logit = keys_scr[rows, :]
            lane = lane_of(ROWS)
            for e in range(experts):
                part = every_ref[rows, e * LANES : (e + 1) * LANES].astype(F32)
                total = jnp.sum(value_grad * part, axis=1, keepdims=True)
                logit = jnp.where(lane == head_dim + e, total, logit)
            key_grad = jnp.where(real, logit, logit * gates * (1.0 - gates)).astype(BF16)
            key_grad_ref[rows, :] = key_grad

            @pl.when(block * ROWS >= mem)
            def _():
                place = block - mem // ROWS
                slot = place ^ z_ref[0]
                value_pack = jnp.where(real, value_grad, gates).astype(BF16)
                for side, pack_ref in enumerate(pack_refs):

                    @pl.when(slot // 2 == side)
                    def _():
                        pack_ref[slot % 2, 0] = key_grad
                        pack_ref[slot % 2, 1] = value_pack
                        pack_ref[slot % 2, 2] = query_scr[pl.ds(place * ROWS, ROWS), :]


def attend_back(
    rank,
    qc,
    qp,
    key_vecs,
    value_vecs,
    rel_reverse,
    probs,
    heads,
    ogate,
    every,
    vgate,
    backs,
    head_dim,
):
    toks = qc.shape[0]
    keys = key_vecs.shape[0]
    span = rel_reverse.shape[0]
    steps = toks // ROWS
    wide = span + ROWS
    experts = every.shape[1] // LANES
    row = lambda i, z: (i, 0)
    return pl.pallas_call(
        functools.partial(attend_back_kernel, span, experts, head_dim, steps),
        grid_spec=pltpu.PrefetchScalarGridSpec(
            num_scalar_prefetch=1,
            grid=(steps,),
            in_specs=[
                pl.BlockSpec((ROWS, LANES), row),
                pl.BlockSpec((ROWS, LANES), row),
                whole(keys, LANES),
                whole(keys, LANES),
                whole(span, LANES),
                pl.BlockSpec((ROWS, wide), row),
                pl.BlockSpec((ROWS, LANES), row),
                pl.BlockSpec((ROWS, LANES), row),
                whole(keys, experts * LANES),
                whole(keys, LANES),
            ]
            + [whole(2, ROWS, LANES)] * (steps // 2),
            out_specs=[
                whole(keys, LANES),
                whole(keys, LANES),
                pl.BlockSpec((ROWS, LANES), row),
                whole(span, LANES),
                whole(2, LANES),
            ]
            + [whole(2, 3, ROWS, LANES)] * (steps // 2),
            scratch_shapes=[
                pltpu.VMEM((keys, LANES), F32),
                pltpu.VMEM((keys, LANES), F32),
                pltpu.VMEM((span, LANES), F32),
                pltpu.VMEM((toks, LANES), BF16),
                pltpu.VMEM((ROWS, LANES), BF16),
            ],
        ),
        out_shape=[
            struct((keys, LANES), BF16),
            struct((keys, LANES), F32),
            struct((toks, LANES), BF16),
            struct((span, LANES), BF16),
            struct((2, LANES), F32),
        ]
        + [struct((2, 3, ROWS, LANES), BF16)] * (steps // 2),
        compiler_params=params(),
        cost_estimate=cost(15),
        name="attend_back",
    )(rank, qc, qp, key_vecs, value_vecs, rel_reverse, probs, heads, ogate, every, vgate, *backs)


def mix_kernel(experts, head_dim, where_ref, *refs):
    pack_refs, refs = refs[:2], refs[2:]
    own_ref, even_ref, odd_ref, full_ref, own_part_ref, near_part_ref, mixed_scr = refs
    step = pl.program_id(0)

    @pl.when(step == 0)
    def _():
        real = lane_of(ROWS) < head_dim
        for h in range(2):
            for block in range(2):
                pack = pack_refs[h][block].astype(F32)
                out = jnp.where(real, pack, 0.0)
                rows = slice(block * ROWS, (block + 1) * ROWS)
                for e in range(experts):
                    gate = pack[:, head_dim + e : head_dim + e + 1]
                    mixed_scr[h, rows, e * LANES : (e + 1) * LANES] = (gate * out).astype(BF16)

    turned = where_ref[1] == 1
    even, odd = even_ref[0], odd_ref[0]
    far = jnp.concatenate([jnp.where(turned, odd, even), jnp.where(turned, even, odd)], axis=1)
    total = None
    for h, weight in enumerate((own_ref[...], far)):
        for e in range(experts):
            full_ref[h, e * LANES : e * LANES + head_dim, :] = weight[
                e * head_dim : (e + 1) * head_dim
            ]
            full_ref[h, e * LANES + head_dim : (e + 1) * LANES, :] = jnp.zeros(
                (LANES - head_dim, weight.shape[1]), BF16
            )
        part = mm(mixed_scr[h], full_ref[h])
        total = part if total is None else total + part
    own_part_ref[...] = total[:ROWS]
    near_part_ref[...] = total[ROWS:].astype(BF16)


def mix(where, packs, own_weight, even, odd, experts, head_dim):
    depth, width = own_weight.shape
    steps = even.shape[0]
    size = width // steps
    column = lambda s, w: (0, w[0] ^ s)
    return pl.pallas_call(
        functools.partial(mix_kernel, experts, head_dim),
        grid_spec=pltpu.PrefetchScalarGridSpec(
            num_scalar_prefetch=1,
            grid=(steps,),
            in_specs=[whole(2, ROWS, LANES)] * 2
            + [
                pl.BlockSpec((depth, size), column),
                pl.BlockSpec((1,) + even.shape[1:], lambda s, w: (s, 0, 0)),
                pl.BlockSpec((1,) + odd.shape[1:], lambda s, w: (s, 0, 0)),
            ],
            out_specs=[
                pl.BlockSpec((2, experts * LANES, size), lambda s, w: (0, 0, w[0] ^ s)),
                pl.BlockSpec((ROWS, size), column),
                pl.BlockSpec((ROWS, size), column),
            ],
            scratch_shapes=[pltpu.VMEM((2, 2 * ROWS, experts * LANES), BF16)],
        ),
        out_shape=[
            struct((2, experts * LANES, width), BF16),
            struct((ROWS, width), F32),
            struct((ROWS, width), BF16),
        ],
        compiler_params=params(),
        cost_estimate=cost(7),
        name="mix",
    )(where, *packs, own_weight, even, odd)


def middle_kernel(z_ref, tok_ref, own_ref, near_ref, gain_ref, bias_ref, middle_ref, up_ref):
    middle = tok_ref[...].astype(F32) + (own_ref[...] + near_ref[...].astype(F32))
    middle_ref[...] = middle
    normal, _ = norm_parts(middle)
    up_ref[...] = (normal * gain_ref[...] + bias_ref[...]).astype(BF16)


def middle_rows(rank, tokens, own, near, gain, bias):
    rows, width = own.shape
    steps = 2
    block = pl.BlockSpec((rows // steps, width), lambda i, z: (i, 0))
    return pl.pallas_call(
        middle_kernel,
        grid_spec=pltpu.PrefetchScalarGridSpec(
            num_scalar_prefetch=1,
            grid=(steps,),
            in_specs=[
                pl.BlockSpec((rows // steps, width), lambda i, z: (z[0] * steps + i, 0)),
                block,
                block,
                whole(1, width),
                whole(1, width),
            ],
            out_specs=[block, block],
        ),
        out_shape=[struct((rows, width), F32), struct((rows, width), BF16)],
        compiler_params=params(),
        cost_estimate=cost(3),
        name="middle",
    )(rank, tokens, own, near, gain, bias)


def middle_back_kernel(
    own_ref, near_ref, cot_ref, middle_ref, gain_ref, grad_ref, low_ref, sums_ref
):
    upstream = own_ref[...].astype(F32) + near_ref[...].astype(F32)
    normal, inv_std = norm_parts(middle_ref[...])

    @pl.when(pl.program_id(0) == 0)
    def _():
        sums_ref[...] = jnp.zeros_like(sums_ref)

    sums_ref[0:1, :] += jnp.sum(upstream * normal, axis=0, keepdims=True)
    sums_ref[1:2, :] += jnp.sum(upstream, axis=0, keepdims=True)
    grad = cot_ref[...].astype(F32) + norm_back(upstream, normal, inv_std, gain_ref[...])
    grad_ref[...] = grad
    low_ref[...] = grad.astype(BF16)


def middle_back(own, near, cot, middle, gain):
    rows, width = middle.shape
    steps = 2
    block = pl.BlockSpec((rows // steps, width), lambda i: (i, 0))
    return pl.pallas_call(
        middle_back_kernel,
        grid=(steps,),
        in_specs=[block] * 4 + [whole(1, width)],
        out_specs=[block, block, whole(2, width)],
        out_shape=[
            struct((rows, width), F32),
            struct((rows, width), BF16),
            struct((2, width), F32),
        ],
        compiler_params=params(),
        cost_estimate=cost(4),
        name="middle_back",
    )(own, near, cot, middle, gain)


def heads_back_kernel(experts, head_dim, own_ref, near_ref, full_ref, *refs):
    pack_refs, out_refs = refs[:2], refs[2:]
    lane = lane_of(ROWS)
    real = lane < head_dim
    grads = [mm_nt(ref[...], full_ref[0]) for ref in (own_ref, near_ref)]
    for h in range(2):

        @pl.when(pl.program_id(0) == h)
        def _():
            for block, grad in enumerate(grads):
                grad = grad.astype(BF16).astype(F32)
                pack = pack_refs[h][block].astype(F32)
                total = jnp.zeros((ROWS, LANES), F32)
                gates = jnp.zeros((ROWS, LANES), F32)
                for e in range(experts):
                    part = grad[:, e * LANES : (e + 1) * LANES]
                    total = total + pack[:, head_dim + e : head_dim + e + 1] * part
                    inner = jnp.sum(part * pack, axis=1, keepdims=True)
                    gates = jnp.where(lane == head_dim + e, inner, gates)
                out_refs[h][block] = jnp.where(real, total, gates).astype(BF16)


def heads_back(own, near, full, packs, experts, head_dim):
    heads, depth, width = full.shape
    rows = own.shape[0]
    return pl.pallas_call(
        functools.partial(heads_back_kernel, experts, head_dim),
        grid=(heads,),
        in_specs=[whole(rows, width)] * 2
        + [pl.BlockSpec((1, depth, width), lambda m: (m, 0, 0))]
        + [whole(2, ROWS, LANES)] * 2,
        out_specs=[whole(2, ROWS, LANES)] * 2,
        out_shape=[struct((2, ROWS, LANES), BF16)] * 2,
        compiler_params=params(),
        cost_estimate=cost(6),
        name="heads_back",
    )(own, near, full, *packs)


def feed_kernel(half, up_ref, cot_ref, wu_ref, wd_ref, far_u_ref, far_d_ref, *refs):
    refs = refs[-6:]
    hidden_ref, pre_grad_ref, out_ref, up_grad_ref, out_scr, up_scr = refs
    step = pl.program_id(0)
    steps = pl.num_programs(0)
    width = up_ref.shape[1]
    count = wu_ref.shape[1] // ROWS

    @pl.when(step == 0)
    def _():
        out_scr[...] = jnp.zeros_like(out_scr)
        up_scr[...] = jnp.zeros_like(up_scr)

    def part(w_up, w_down):
        pres, grads = [], []
        for b in range(count):
            cols = slice(b * ROWS, (b + 1) * ROWS)
            pres.append(mm(up_ref[...], w_up[:, cols]))
            grads.append(mm_nt(cot_ref[...], w_down[cols, :]))
        out, up_grad = None, None
        for b in range(count):
            cols = slice(b * ROWS, (b + 1) * ROWS)
            pre = pres[b]
            hidden_grad = grads[b].astype(BF16).astype(F32)
            phi = 0.5 * (1.0 + lax.erf(pre * ROOT_HALF))
            hidden = (pre * phi).astype(BF16)
            slope = phi + pre * jnp.exp(-0.5 * pre * pre) * INVERSE_ROOT_TAU
            pre_grad = (hidden_grad * slope).astype(BF16)
            hidden_ref[:, cols] = hidden
            pre_grad_ref[:, cols] = pre_grad
            out_part, up_part = mm(hidden, w_down[cols, :]), mm_nt(pre_grad, w_up[:, cols])
            out = out_part if out is None else out + out_part
            up_grad = up_part if up_grad is None else up_grad + up_part
        out_scr[...] += out
        up_scr[...] += up_grad

    @pl.when(step < half)
    def _():
        part(wu_ref[...], wd_ref[...])

    @pl.when(step >= half)
    def _():
        part(far_u_ref[...].reshape(width, -1), far_d_ref[...].reshape(-1, width))

    @pl.when(step == steps - 1)
    def _():
        out_ref[...] = out_scr[...].astype(out_ref.dtype)
        up_grad_ref[...] = up_scr[...].astype(up_grad_ref.dtype)


def feed(up_in, cot, w_up, w_down, far, dtype, *deps):
    rows, width = up_in.shape
    hidden = w_up.shape[1]
    size = 2 * ROWS
    half = hidden // size
    pieces, _, depth, _ = far.shape
    count = size // depth
    own = lambda i: jnp.minimum(i, half - 1)
    other = lambda i: jnp.maximum(i - half, 0)
    return pl.pallas_call(
        functools.partial(feed_kernel, half),
        grid=(2 * half,),
        in_specs=[
            whole(rows, width),
            whole(rows, width),
            pl.BlockSpec((width, size), lambda i: (0, own(i))),
            pl.BlockSpec((size, width), lambda i: (own(i), 0)),
            pl.BlockSpec((pieces, 1, depth, size), lambda i: (0, 0, 0, other(i))),
            pl.BlockSpec((count, 1, depth, width), lambda i: (other(i), 1, 0, 0)),
        ]
        + [pl.BlockSpec(memory_space=pl.ANY)] * len(deps),
        out_specs=[
            pl.BlockSpec((rows, size), lambda i: (0, i)),
            pl.BlockSpec((rows, size), lambda i: (0, i)),
            whole(rows, width),
            whole(rows, width),
        ],
        out_shape=[
            struct((rows, 2 * hidden), BF16),
            struct((rows, 2 * hidden), BF16),
            struct((rows, width), dtype),
            struct((rows, width), dtype),
        ],
        scratch_shapes=[pltpu.VMEM((rows, width), F32), pltpu.VMEM((rows, width), F32)],
        compiler_params=params(),
        cost_estimate=cost(10),
        name="feed",
    )(up_in, cot, w_up, w_down, far, far, *deps)


def feed_weights_kernel(count, half, *refs):
    lefts, refs = refs[: 2 * count], refs[2 * count :]
    rights, out_ref = refs[: 2 * count], refs[2 * count]
    step = pl.program_id(0)

    for which in range(2):

        @pl.when((step // half) % 2 == which)
        def _():
            total = None
            for m in range(which * count, (which + 1) * count):
                part = mm_tn(lefts[m][...], rights[m][...])
                total = part if total is None else total + part
            out_ref[...] = total.astype(BF16)


def feed_weights(ups, cots, pre_grads, hiddens):
    count = len(ups)
    rows, width = ups[0].shape
    hidden = hiddens[0].shape[1] // 2
    size = 512
    half = hidden // size

    def columns(which):
        def at(i):
            shard, inner = i // (2 * half), i % (2 * half)
            return (0, shard * half + jnp.clip(inner - which * half, 0, half - 1))

        return pl.BlockSpec((rows, size), at)

    return pl.pallas_call(
        functools.partial(feed_weights_kernel, count, half),
        grid=(4 * half,),
        in_specs=[whole(rows, width)] * (2 * count)
        + [columns(0)] * count
        + [columns(1)] * count,
        out_specs=pl.BlockSpec((width, size), lambda i: (0, i)),
        out_shape=struct((width, 4 * hidden), BF16),
        compiler_params=params(),
        cost_estimate=cost(11),
        name="feed_weights",
    )(*ups, *cots, *pre_grads, *hiddens)


def out_weights_kernel(experts, head_dim, heads, where_ref, *refs):
    pack_refs, refs = refs[:heads], refs[heads:]
    grad_ref, near_grad_ref, keep_ref, send_ref, mixed_scr, scr = refs
    real = lane_of(ROWS) < head_dim

    def fill(begin, pack):
        pack = pack.astype(F32)
        out = jnp.where(real, pack, 0.0)
        for e in range(experts):
            gate = pack[:, head_dim + e : head_dim + e + 1]
            mixed_scr[begin : begin + ROWS, e * LANES : (e + 1) * LANES] = (gate * out).astype(
                BF16
            )

    for m in range(heads):

        @pl.when(pl.program_id(0) == m)
        def _():
            fill(0, pack_refs[m][0])
            fill(ROWS, pack_refs[m][1])

    scr[...] = mm_tn(mixed_scr[:ROWS], grad_ref[...]) + mm_tn(
        mixed_scr[ROWS:], near_grad_ref[...]
    )
    for k in range(GROUP):
        target = send_ref if k % 2 else keep_ref
        lanes = pl.ds(pl.multiple_of((where_ref[0] ^ k) * LANES, LANES), LANES)
        for e in range(experts):
            target[k // 2, e * head_dim : (e + 1) * head_dim, :] = scr[
                e * LANES : e * LANES + head_dim, lanes
            ].astype(BF16)


def out_weights(where, packs, grad, near_grad, experts, head_dim):
    heads = len(packs)
    rows, width = grad.shape
    depth = experts * head_dim
    shape = (GROUP // 2, heads * depth, width // GROUP)
    spec = pl.BlockSpec((GROUP // 2, depth, width // GROUP), lambda m, w: (0, m, 0))
    return pl.pallas_call(
        functools.partial(out_weights_kernel, experts, head_dim, heads),
        grid_spec=pltpu.PrefetchScalarGridSpec(
            num_scalar_prefetch=1,
            grid=(heads,),
            in_specs=[whole(2, rows, LANES)] * heads + [whole(rows, width)] * 2,
            out_specs=[spec] * 2,
            scratch_shapes=[
                pltpu.VMEM((2 * rows, experts * LANES), BF16),
                pltpu.VMEM((experts * LANES, width), F32),
            ],
        ),
        out_shape=[struct(shape, BF16)] * 2,
        compiler_params=params(),
        cost_estimate=cost(5),
        name="out_weights",
    )(where, *packs, grad, near_grad)


def weights_kernel(
    experts,
    head_dim,
    counts,
    where_ref,
    normed_ref,
    key_ref,
    value_ref,
    gate_ref,
    query_ref,
    table_ref,
    rel_ref,
    w_ref,
    gain_ref,
    bias_ref,
    sums_ref,
    biases_ref,
    keep_ref,
    send_ref,
    small_ref,
    grads_scr,
    sum_scr,
    main_scr,
    rel_scr,
):
    step = pl.program_id(0)
    mem_steps, key_steps, rel_steps = counts
    query = (1 + experts) * LANES

    @pl.when(step == 0)
    def _():
        main_scr[...] = jnp.zeros_like(main_scr)
        sum_scr[...] = jnp.zeros_like(sum_scr)
        rel_scr[...] = jnp.zeros_like(rel_scr)

    def add(columns):
        grads = grads_scr[:, :columns]
        main_scr[:columns, :] += mm_tn(grads, normed_ref[...])
        sum_scr[0:1, :columns] += jnp.sum(grads.astype(F32), axis=0, keepdims=True)

    @pl.when(step < key_steps)
    def _():
        value_grad = value_ref[...]
        grads_scr[:, :LANES] = key_ref[...]
        for e in range(experts):
            gate = gate_ref[:, head_dim + e : head_dim + e + 1]
            grads_scr[:, LANES * (1 + e) : LANES * (2 + e)] = (gate * value_grad).astype(BF16)

    @pl.when(step < mem_steps)
    def _():
        add(query)

    @pl.when((step >= mem_steps) & (step < key_steps))
    def _():
        grads_scr[:, query:] = query_ref[...]
        add(query + LANES)

    @pl.when(step >= key_steps)
    def _():
        rel_scr[...] += mm_tn(rel_ref[...], table_ref[...])

    @pl.when(step == key_steps + rel_steps - 1)
    def _():
        weights = w_ref[...].astype(F32)
        sums = sum_scr[...].T
        bias_one = jnp.sum(weights * sums[:, 0:1], axis=0, keepdims=True)
        inner = jnp.sum(weights * main_scr[...], axis=0, keepdims=True)
        small_ref[...] = jnp.zeros_like(small_ref)
        small_ref[0:1, :] = (inner - bias_ref[...] * bias_one) / gain_ref[...]
        small_ref[1:2, :] = bias_one
        small_ref[2:4, :] = sums_ref[...]
        small_ref[4:6, pl.ds(pl.multiple_of(where_ref[1] * LANES, LANES), LANES)] = biases_ref[...]
        for k in range(GROUP):
            target = send_ref if k % 2 else keep_ref
            at = k // 2
            lanes = pl.ds(pl.multiple_of((where_ref[0] ^ k) * LANES, LANES), LANES)
            row = 0

            def put(source, begin, size):
                target[at, row : row + size, :] = source[begin : begin + size, lanes].astype(BF16)
                return row + size

            for section in range(2 + experts):
                row = put(main_scr, section * LANES, head_dim)
            row = put(rel_scr, 0, head_dim)
            target[at, row:, :] = jnp.concatenate(
                [
                    main_scr[head_dim : head_dim + 8, lanes],
                    main_scr[query + head_dim : query + head_dim + 8, lanes],
                ],
                axis=0,
            ).astype(BF16)


def weight_grads(
    where,
    normed,
    key_grad,
    value_grad,
    gates,
    query_grad,
    table,
    rel_grad,
    w_all,
    gain,
    bias,
    sums_two,
    bias_sums,
    mem,
    head_dim,
    experts,
):
    keys, width = normed.shape
    cols = (2 + experts) * LANES
    big = 4 * ROWS
    mem_steps, key_steps = mem // big, keys // big
    rel_steps = table.shape[0] // big
    counts = (mem_steps, key_steps, rel_steps)
    rows = (3 + experts) * head_dim + 16
    key_row = lambda i, w: (jnp.minimum(i, key_steps - 1), 0)
    tok_row = lambda i, w: (jnp.clip(i - mem_steps, 0, key_steps - mem_steps - 1), 0)
    rel_row = lambda i, w: (jnp.clip(i - key_steps, 0, rel_steps - 1), 0)
    half = GROUP // 2
    return pl.pallas_call(
        functools.partial(weights_kernel, experts, head_dim, counts),
        grid_spec=pltpu.PrefetchScalarGridSpec(
            num_scalar_prefetch=1,
            grid=(key_steps + rel_steps,),
            in_specs=[
                pl.BlockSpec((big, width), key_row),
                pl.BlockSpec((big, LANES), key_row),
                pl.BlockSpec((big, LANES), key_row),
                pl.BlockSpec((big, LANES), key_row),
                pl.BlockSpec((big, LANES), tok_row),
                pl.BlockSpec((big, width), rel_row),
                pl.BlockSpec((big, LANES), rel_row),
                whole(cols, width),
                whole(1, width),
                whole(1, width),
                whole(2, width),
                whole(2, LANES),
            ],
            out_specs=[
                whole(half, rows, LANES),
                whole(half, rows, LANES),
                whole(8, width),
            ],
            scratch_shapes=[
                pltpu.VMEM((big, cols), BF16),
                pltpu.VMEM((8, cols), F32),
                pltpu.VMEM((cols, width), F32),
                pltpu.VMEM((LANES, width), F32),
            ],
        ),
        out_shape=[
            struct((half, rows, LANES), BF16),
            struct((half, rows, LANES), BF16),
            struct((8, width), F32),
        ],
        compiler_params=params(),
        cost_estimate=cost(15),
        name="weight_grads",
    )(
        where,
        normed,
        key_grad,
        value_grad,
        gates,
        query_grad,
        table,
        rel_grad,
        w_all,
        gain,
        bias,
        sums_two,
        bias_sums,
    )


def token_kernel(experts, head_dim, own_ref, far_ref, w_own_ref, w_far_ref, *refs):
    out_refs, grads_scr, total_scr = refs[:2], refs[2], refs[3]
    step = pl.program_id(0)
    query = (1 + experts) * LANES
    cols = query + LANES
    real = lane_of(ROWS) < head_dim

    def part(pack_ref, weights):
        for block in range(2):
            rows = slice(block * ROWS, (block + 1) * ROWS)
            value_pack = pack_ref[block, 1].astype(F32)
            value_grad = jnp.where(real, value_pack, 0.0)
            grads_scr[rows, :LANES] = pack_ref[block, 0]
            for e in range(experts):
                gate = value_pack[:, head_dim + e : head_dim + e + 1]
                grads_scr[rows, LANES * (1 + e) : LANES * (2 + e)] = (gate * value_grad).astype(
                    BF16
                )
            grads_scr[rows, query:] = pack_ref[block, 2]
        return mm(grads_scr[...], weights)

    @pl.when(step == 0)
    def _():
        total_scr[...] = part(own_ref, w_own_ref[:cols, :])

    @pl.when(step == 1)
    def _():
        weights = w_far_ref[...].reshape(-1, w_far_ref.shape[2])
        total = total_scr[...] + part(far_ref, weights[:cols, :])
        out_refs[0][...] = total[:ROWS]
        out_refs[1][...] = total[ROWS:].astype(BF16)


def token_parts(own_pack, far_pack, own_w, far_w, head_dim, experts):
    width = own_w.shape[1]
    rows = 2 * ROWS
    cols = (2 + experts) * LANES
    return pl.pallas_call(
        functools.partial(token_kernel, experts, head_dim),
        grid=(2,),
        in_specs=[
            whole(*own_pack.shape),
            whole(*far_pack.shape),
            whole(*own_w.shape),
            whole(*far_w.shape),
        ],
        out_specs=[whole(ROWS, width)] * 2,
        out_shape=[struct((ROWS, width), F32), struct((ROWS, width), BF16)],
        scratch_shapes=[pltpu.VMEM((rows, cols), BF16), pltpu.VMEM((rows, width), F32)],
        compiler_params=params(),
        cost_estimate=cost(6),
        name="token_parts",
    )(own_pack, far_pack, own_w, far_w)


def token_sum_kernel(z_ref, tok_ref, mid_ref, gain_ref, own_ref, near_ref, out_ref):
    total = own_ref[...] + near_ref[...].astype(F32)
    normal, inv_std = norm_parts(tok_ref[...].astype(F32))
    out_ref[...] = mid_ref[...] + norm_back(total, normal, inv_std, gain_ref[...])


def token_sum(rank, tokens, middle_grad, gain, own, near):
    rows, width = middle_grad.shape
    return pl.pallas_call(
        token_sum_kernel,
        grid_spec=pltpu.PrefetchScalarGridSpec(
            num_scalar_prefetch=1,
            grid=(1,),
            in_specs=[
                pl.BlockSpec((rows, width), lambda i, z: (z[0], 0)),
                whole(rows, width),
                whole(1, width),
                whole(rows, width),
                whole(rows, width),
            ],
            out_specs=whole(rows, width),
        ),
        out_shape=struct((rows, width), F32),
        compiler_params=params(),
        cost_estimate=cost(4),
        name="token_sum",
    )(rank, tokens, middle_grad, gain, own, near)


def swap(array, axis, mask):
    size = lax.axis_size(axis)
    return lax.ppermute(array, axis, [(i, i ^ mask) for i in range(size)])


def plus(left, right):
    return (left.astype(F32) + right.astype(F32)).astype(BF16)


def scatter_first(keep, far):
    return [plus(keep[m], far[m]) for m in range(keep.shape[0])]


def scatter_sends(blocks, unit):
    return [swap(blocks[m], "dp", 2 * m * unit) for m in range(1, len(blocks))]


def scatter_done(own, fars, unit, axis):
    out = own.astype(F32)
    for far in fars:
        out = out + far.astype(F32)
    mask = unit // 2
    while mask:
        size = out.shape[axis] // 2
        bit = (lax.axis_index("dp") // mask) % 2
        mine = lax.dynamic_slice_in_dim(out, bit * size, size, axis)
        theirs = lax.dynamic_slice_in_dim(out, (1 - bit) * size, size, axis)
        out = mine + swap(theirs.astype(BF16), "dp", mask).astype(F32)
        mask //= 2
    return out


def spread(far, *gates):
    pieces = [swap(far, "dp", 2 * m) for m in range(1, GROUP // 2)]
    even = after(pile(far, *pieces), *gates)
    odd = swap(even, "dp", 1)
    return even, odd


def on_device(
    tokens,
    memory,
    segments,
    value_routes,
    output_routes,
    first_gain,
    first_bias,
    second_gain,
    second_bias,
    query_head_weight,
    key_weight,
    position_weight,
    value_weight,
    value_select,
    output_expert_selector,
    output_expert_weight,
    content_bias,
    position_bias,
    up_projection_weight,
    down_projection_weight,
    cotangent,
):
    mem_len = memory.shape[1]
    toks, width = tokens.shape
    head_dim = query_head_weight.shape[2]
    experts = value_select.shape[2]
    hidden = up_projection_weight.shape[1]
    parts = lax.axis_size("tensor")
    rank = lax.axis_index("tensor")
    dp = lax.axis_size("dp")
    at = lax.axis_index("dp")
    others = range(1, parts)
    near, far_shard = 1, 2
    rank_ref = rank.reshape(1).astype(jnp.int32)
    row = lambda v: v.reshape(1, -1)
    lanes = lambda v: jnp.pad(v, ((0, 0), (0, LANES - head_dim)))

    own_out = output_expert_weight[0]
    size = width // GROUP
    own_block = lax.dynamic_slice_in_dim(own_out, (at % GROUP) * size, size, 1)
    far_out = swap(own_block, "tensor", far_shard)
    span = mem_len
    fine = 32
    rates = jnp.exp(jnp.arange(width // 2).astype(F32) * (-2.0 * math.log(10000.0) / width))
    coarse_at = (span - 1 - fine * jnp.arange(span // fine)).astype(F32)[:, None] * rates[None, :]
    fine_at = jnp.arange(fine).astype(F32)[:, None] * rates[None, :]
    sin_a, cos_a = jnp.sin(coarse_at)[:, None, :], jnp.cos(coarse_at)[:, None, :]
    sin_b, cos_b = jnp.sin(fine_at)[None, :, :], jnp.cos(fine_at)[None, :, :]
    sin_table = jnp.concatenate(
        [sin_a * cos_b - cos_a * sin_b, cos_a * cos_b + sin_a * sin_b], axis=2
    )
    sin_table = lax.optimization_barrier(sin_table.reshape(span, width).astype(BF16))
    rel_weight = jnp.concatenate(
        [position_weight[0].T, jnp.zeros((LANES - head_dim, width), BF16)]
    )
    rel_reverse = mm_nt(sin_table, rel_weight).astype(BF16)

    w_all, normed, key_vecs, value_vecs, every, vgate, qc, qp, ogate = project(
        memory[0],
        tokens,
        row(first_gain),
        row(first_bias),
        (
            key_weight[0].T,
            value_select[0].T,
            value_weight[0].T,
            query_head_weight[0].T,
            output_expert_selector[0].T,
        ),
        value_routes[0, :, 0].T,
        output_routes[:, 0].T,
        lanes(content_bias),
        lanes(position_bias),
        experts,
        head_dim,
    )
    steps = toks // ROWS
    seg = segments[0]
    seg_keys = jnp.stack([seg[i * ROWS : i * ROWS + span + ROWS] for i in range(steps)])[:, None]
    seg_keys = after(seg_keys, far_out)
    heads, probs, *packs = attend(
        rank_ref,
        qc,
        qp,
        key_vecs,
        value_vecs,
        rel_reverse,
        seg_keys,
        seg[mem_len:, None],
        ogate,
        head_dim,
    )

    depth = width // dp
    feed_piece = jnp.stack(
        [
            lax.dynamic_slice_in_dim(up_projection_weight, at * depth, depth, 0),
            lax.dynamic_slice_in_dim(down_projection_weight, at * (hidden // dp), hidden // dp, 0),
        ]
    )
    far_feed = swap(feed_piece, "tensor", far_shard)
    far_feed = lax.all_gather(after(far_feed, packs[0]), "dp", axis=0)
    packs = [packs[0], swap(packs[1], "tensor", far_shard)]
    even, odd = spread(after(far_out, qc), packs[1])
    cots = [cotangent, swap(after(cotangent, packs[1]), "tensor", near)]
    piece = w_all.shape[0] // dp
    own_piece = lax.dynamic_slice_in_dim(w_all, at * piece, piece, 0)
    far_w = swap(after(own_piece, packs[1]), "tensor", far_shard)
    group_at = at % GROUP
    where = jnp.stack([group_at // 2, group_at % 2, rank]).astype(jnp.int32)
    full, own_part, near_part = mix(where, packs, own_out, even, odd, experts, head_dim)
    middle, up_in = middle_rows(
        rank_ref,
        tokens,
        after(own_part, far_w, cots[1]),
        swap(near_part, "tensor", near),
        row(second_gain),
        row(second_bias),
    )

    ups = [up_in, swap(up_in, "tensor", near)]
    unit = dp // GROUP
    where_grads = jnp.stack([at // unit, rank]).astype(jnp.int32)
    far_w = lax.all_gather(after(far_w, up_in), "dp", axis=0)
    shards = (up_projection_weight, down_projection_weight, far_feed)
    own_hidden, own_pre, own_result, own_up = feed(ups[0], cots[0], *shards, F32)
    near_hidden, near_pre, near_result, near_up = feed(ups[1], cots[1], *shards, BF16, own_pre)
    back_up = swap(near_up, "tensor", near)
    feed_sums = feed_weights(ups, cots, (own_pre, near_pre), (own_hidden, near_hidden))
    feed_sums = after(feed_sums, far_w, back_up)
    own_up = after(own_up, feed_sums)
    feed_sums = lax.psum_scatter(feed_sums, "dp", scatter_dimension=0, tiled=True)

    middle_grad, attn_grad, sums_two = middle_back(
        own_up, back_up, cotangent, middle, row(second_gain)
    )
    near_grad = swap(attn_grad, "tensor", near)
    backs = heads_back(attn_grad, near_grad, full, packs, experts, head_dim)
    out_keep, out_send = out_weights(where_grads, packs, attn_grad, near_grad, experts, head_dim)
    backs = [after(backs[0], out_keep), swap(backs[1], "tensor", far_shard)]
    back_out = swap(after(near_result, backs[1]), "tensor", near)

    key_grad, value_grad, query_grad, rel_grad, bias_sums, *grad_packs = attend_back(
        rank_ref,
        qc,
        qp,
        key_vecs,
        value_vecs,
        rel_reverse,
        probs,
        heads,
        ogate,
        every,
        vgate,
        backs,
        head_dim,
    )
    out_part = scatter_first(out_keep, swap(out_send, "dp", unit))
    rel_grad = after(rel_grad, *out_part, back_out)
    out_fars = scatter_sends(out_part, unit)
    far_pack = swap(grad_packs[1], "tensor", far_shard)
    keep, send, small = weight_grads(
        where_grads,
        normed,
        key_grad,
        value_grad,
        vgate,
        query_grad,
        sin_table,
        rel_grad,
        w_all,
        row(first_gain),
        row(first_bias),
        sums_two,
        bias_sums,
        mem_len,
        head_dim,
        experts,
    )
    token_own, token_near = token_parts(
        grad_packs[0], far_pack, w_all, after(far_w, keep), head_dim, experts
    )
    send, small = (after(each, token_near, span=20) for each in (send, small))
    token_near = swap(token_near, "tensor", near)
    kept_far = swap(send, "dp", unit)
    small_fars = [swap(small, "tensor", m) for m in others]
    out_fars = [after(far, send) for far in out_fars]
    out_sums = scatter_done(out_part[0], out_fars, unit, 1).reshape(2, experts * head_dim, -1)
    out_low = out_sums[1].astype(BF16)
    feed_own, feed_far = feed_sums[:, : 2 * hidden], feed_sums[:, 2 * hidden :]
    kept_far, feed_far, *small_fars = together(kept_far, feed_far, *small_fars)
    feed_far = swap(feed_far, "tensor", far_shard)
    out_far = swap(out_low, "tensor", far_shard)
    kept = scatter_first(keep, kept_far)
    for far in small_fars:
        small = small + far
    kept_fars = scatter_sends(kept, unit)
    small_fars = [swap(small, "dp", m) for m in range(2, GROUP, 2)]
    feed_far, *fars = together(feed_far, *kept_fars, *small_fars)
    kept_fars, small_fars = fars[: len(fars) // 2], fars[len(fars) // 2 :]
    for far in small_fars:
        small = small + far
    mask = GROUP
    while mask < dp:
        small = small + swap(small, "dp", mask)
        mask *= 2
    small = small + swap(small, "dp", 1)
    kept = scatter_done(kept[0], kept_fars, unit, 1)
    tokens_grad = token_sum(
        rank_ref, tokens, middle_grad, row(first_gain), token_own, token_near
    )
    result = (middle + own_result + after(back_out, keep).astype(F32)).astype(BF16)
    out_w = out_sums[0] + after(out_far, *kept_fars).astype(F32)
    feed_grads = feed_own.astype(F32) + feed_far.astype(F32)
    up_total = feed_grads[:, :hidden]
    down_total = feed_grads[:, hidden:].T
    biases = small[4:6, : parts * LANES].reshape(2, parts, LANES)[:, :, :head_dim]
    marks = [0, 1, 1 + experts, 2 + experts, 3 + experts]
    key_w, value_w, query_w, rel_w = (
        kept[a * head_dim : b * head_dim] for a, b in zip(marks, marks[1:])
    )
    select = marks[-1] * head_dim
    turn = lambda part: part.T[None]
    return (
        result,
        tokens_grad,
        small[0],
        small[1],
        small[2],
        small[3],
        turn(query_w),
        turn(key_w),
        turn(rel_w),
        turn(value_w),
        turn(kept[select : select + experts]),
        turn(kept[select + 8 : select + 8 + experts]),
        out_w[None],
        biases[0],
        biases[1],
        up_total,
        down_total,
    )


def solution(mesh):
    placed = (
        P("dp", None),
        P("dp", None, None),
        P("dp", None),
        P("dp", None, "tensor", None),
        P("dp", "tensor", None),
        P(),
        P(),
        P(),
        P(),
        P("tensor", None, None),
        P("tensor", None, None),
        P("tensor", None, None),
        P("tensor", None, None),
        P("tensor", None, None),
        P("tensor", None, None),
        P("tensor", None, None),
        P("tensor", None),
        P("tensor", None),
        P(None, "tensor"),
        P("tensor", None),
        P(("dp", "tensor"), None),
    )
    return jax.shard_map(
        on_device,
        mesh=mesh,
        in_specs=placed,
        out_specs=(
            P(("dp", "tensor"), None),
            P(("dp", "tensor"), None),
            P(),
            P(),
            P(),
            P(),
            P("tensor", "dp", None),
            P("tensor", "dp", None),
            P("tensor", "dp", None),
            P("tensor", "dp", None),
            P("tensor", "dp", None),
            P("tensor", "dp", None),
            P("tensor", None, "dp"),
            P(),
            P(),
            P("dp", "tensor"),
            P("tensor", "dp"),
        ),
        check_vma=False,
    )
```

profile of v0, /device:TPU:0, one launch (start us, length us, event | category | flops | bytes accessed | tf_op | source)
XLA Modules:
  0.0 273.0 jit_solution(7687043853380355393)
XLA Ops:
  7.3 0.9 dynamic-slice_bitcast_fusion.2
  8.2 4.1 %collective-permute-start = (bf16[560,128]{1,0:T(8,128)(2,1)S(1)}, bf16[560,128]{1,0:T(8,128)(2,1)S(1)}, u32[]{:S(2)}, u32[]{:S(2)}) collective-permute-start(bf16[560,128]{1,0:T(8,128)(2,1)S(1)} %dynamic-slice_bitcast_fusion.2), channel_id=1, source_target_pairs={{0,2},{1,3},{2,0},{3,1},{4,6},{5,7},{6,4},{7,5},{8,10},{9,11},{10,... | collective-permute-start | bytes 430088 | tf_op jit(solution)/shard_map/ppermute | solution.py:1159
  12.3 1.1 dynamic-slice_bitcast_fusion
  13.4 0.9 pad_maximum_fusion.1
  16.0 1.0 copy.78.segq_ref
  18.3 1.6 pad_maximum_fusion.table_ref
  19.9 11.4 %project.1 = (bf16[1024,1024]{1,0:T(8,128)(2,1)}, bf16[2048,1024]{1,0:T(8,128)(2,1)}, bf16[2048,128]{1,0:T(8,128)(2,1)}, bf16[2048,128]{1,0:T(8,128)(2,1)}, bf16...) custom-call(bf16[1024,1024]{1,0:T(8,128)(2,1)} %bitcast.116, ...), custom_call_target="tpu_custom_call" | custom-call | flops 13799999488 | tf_op jit(solution)/shard_map/project/pallas_call | solution.py:220
  31.3 3.0 %convolution_convert_fusion.rel_ref = bf16[1024,128]{1,0:T(8,128)(2,1)} fusion(bf16[1024,1024]{1,0:T(8,128)(2,1)} %pad_maximum_fusion.table_ref, bf16[112,1024]{1,0:T(8,128)(2,1)} %bitcast.106), kind=kOutput, calls=%fused_computation.3 | convolution fusion | flops 268566528 | bytes 2588672 | tf_op jit(solution)/shard_map/dot_general | solution.py:26
  35.0 7.7 %attend.1 = (f32[1024,128]{1,0:T(8,128)}, bf16[1024,1280]{1,0:T(8,128)(2,1)}, bf16[2,256,128]{2,1,0:T(8,128)(2,1)}, bf16[2,256,128]{2,1,0:T(8,128)(2,1)}) custom-call(s32[1]{0:T(128)} %bitcast.z_ref, bf16[1024,128]{1,0:T(8,128)(2,1)} %get-tuple-element.74.qc_ref.refs_1_, bf16[1024,128]{1,0:T(8,128)(2,1)} %get-tuple-element.75.qp_ref, ...), custom_call_target="tpu_custom_call" | custom-call | flops 9200000000 | tf_op jit(solution)/shard_map/attend/pallas_call | solution.py:319
  42.7 0.8 copy-done.5
  43.7 2.8 %collective-permute-start.4 = (bf16[560,128]{1,0:T(8,128)(2,1)}, bf16[560,128]{1,0:T(8,128)(2,1)S(1)}, u32[]{:S(2)}, u32[]{:S(2)}) collective-permute-start(bf16[560,128]{1,0:T(8,128)(2,1)} %after.22.refs_0_), channel_id=1, source_target_pairs={{0,24},{4,28},{8,16},{12,20},{16,8},{20,12},{24,0},{28,4},{1,25},{... | collective-permute-start | bytes 430088 | tf_op jit(solution)/shard_map/ppermute | solution.py:1159
  47.2 2.9 %collective-permute-start.1 = (bf16[2,256,128]{2,1,0:T(8,128)(2,1)}, bf16[2,256,128]{2,1,0:T(8,128)(2,1)S(1)}, u32[]{:S(2)}, u32[]{:S(2)}) collective-permute-start(bf16[2,256,128]{2,1,0:T(8,128)(2,1)} %get-tuple-element.80), channel_id=1, source_target_pairs={{0,2},{1,3},{2,0},{3,1},{4,6},{5,7},{6,4},{7,5},{8,10},{9,11},{10,... | collective-permute-start | bytes 393224 | tf_op jit(solution)/shard_map/ppermute | solution.py:1159
  50.8 2.4 collective-permute-done.3.refs_2_
  53.3 2.0 pile.1.refs_0_
  56.0 0.8 copy.86.refs_0_
  57.5 1.6 collective-permute-start.7
  59.1 6.4 %mix.1 = (bf16[2,640,1024]{2,1,0:T(8,128)(2,1)}, f32[256,1024]{1,0:T(8,128)}, bf16[256,1024]{1,0:T(8,128)(2,1)}) custom-call(s32[3]{0:T(128)} %pad_add_fusion.1.where_ref, bf16[2,256,128]{2,1,0:T(8,128)(2,1)} %get-tuple-element.79.refs_0_.refs_1_, bf16[2,256,128]{2,1,0:T(8,128)(2,1)} %copy-done.8, bf16[560,1024]{1,0:T(8,128)(2,1)} %bitcast.107, ...), custom_call_target="tpu_custom_call" | custom-call | flops 8049999872 | tf_op jit(solution)/shard_map/mix/pallas_call | solution.py:565
  65.5 0.9 collective-permute-start.8
  66.4 1.7 constant_dynamic-slice_fusion.refs_0_
  68.1 2.6 collective-permute-start.6
  70.7 17.4 %collective-permute-done.6.refs_1_.refs_0_ = bf16[128,1024]{1,0:T(8,128)(2,1)S(1)} collective-permute-done((bf16[128,1024]{1,0:T(8,128)(2,1)}, bf16[128,1024]{1,0:T(8,128)(2,1)S(1)}, u32[]{:S(2)}, u32[]{:S(2)}) %collective-permute-start.6) | collective-permute-done | bytes 262176 | tf_op jit(solution)/shard_map/ppermute | solution.py:1159
  89.0 2.5 middle.1
  91.8 3.4 %collective-permute-start.10 = (bf16[256,1024]{1,0:T(8,128)(2,1)}, bf16[256,1024]{1,0:T(8,128)(2,1)S(1)}, u32[]{:S(2)}, u32[]{:S(2)}) collective-permute-start(bf16[256,1024]{1,0:T(8,128)(2,1)} %get-tuple-element.85.up_ref.refs_0_.refs_1_), channel_id=1, source_target_pairs={{0,1},{1,0},{2,3},{3,2},{4,5},{5,4},{6,7},{7,6},{8,9},{9,8},{10,11... | collective-permute-start | bytes 1572872 | tf_op jit(solution)/shard_map/ppermute | solution.py:1159
  95.3 10.4 %feed.2 = (bf16[256,2048]{1,0:T(8,128)(2,1)}, bf16[256,2048]{1,0:T(8,128)(2,1)}, f32[256,1024]{1,0:T(8,128)}, f32[256,1024]{1,0:T(8,128)}) custom-call(bf16[256,1024]{1,0:T(8,128)(2,1)} %get-tuple-element.85.up_ref.refs_0_.refs_1_, bf16[256,1024]{1,0:T(8,128)(2,1)} %cot_ref.3, bf16[1024,1024]{1,0:T(8,128)(2,1)} %wu_ref.3, bf16[1024,1024]{1,0:T(8,128)(2,1)} %wd_ref.3, ...), custom_call_target="tpu_custom_call" | custom-call | flops 11500000256 | tf_op jit(solution)/shard_map/feed/pallas_call | solution.py:761
  105.7 1.6 collective-permute-done.10.up_ref.refs_1_
  107.3 0.8 copy-done.28
  108.1 10.1 %feed.3 = (bf16[256,2048]{1,0:T(8,128)(2,1)}, bf16[256,2048]{1,0:T(8,128)(2,1)}, bf16[256,1024]{1,0:T(8,128)(2,1)}, bf16[256,1024]{1,0:T(8,128)(2,1)}) custom-call(bf16[256,1024]{1,0:T(8,128)(2,1)} %copy-done.28, bf16[256,1024]{1,0:T(8,128)(2,1)} %copy-done.17, bf16[1024,1024]{1,0:T(8,128)(2,1)} %wu_ref.3, bf16[1024,1024]{1,0:T(8,128)(2,1)} %wd_ref.3, ...), custom_call_target="tpu_custom_call" | custom-call | flops 11500000256 | tf_op jit(solution)/shard_map/feed/pallas_call | solution.py:761
  118.2 1.8 collective-permute-start.11
  120.1 11.2 %feed_weights.1.refs_0_ = bf16[1024,4096]{1,0:T(8,128)(2,1)} custom-call(bf16[256,1024]{1,0:T(8,128)(2,1)} %get-tuple-element.85.up_ref.refs_0_.refs_1_, bf16[256,1024]{1,0:T(8,128)(2,1)} %copy-done.28, bf16[256,1024]{1,0:T(8,128)(2,1)} %cot_ref.3, bf16[256,1024]{1,0:T(8,128)(2,1)} %copy-done.17, bf16[256,2048]{1,0:T(8,128)(2,1)} %get-tuple-element.87.refs_0_.refs_4_, ...), custom_call_target="tpu_custom_call" | custom-call | flops 12650000384 | tf_op jit(solution)/shard_map/feed_weights/pallas_call | solution.py:822
  132.4 3.5 %middle_back.1 = (f32[256,1024]{1,0:T(8,128)}, bf16[256,1024]{1,0:T(8,128)(2,1)}, f32[2,1024]{1,0:T(2,128)}) custom-call(f32[256,1024]{1,0:T(8,128)} %after.30.own_ref, bf16[256,1024]{1,0:T(8,128)(2,1)} %copy-done.15, bf16[256,1024]{1,0:T(8,128)(2,1)} %cot_ref.3, f32[256,1024]{1,0:T(8,128)} %get-tuple-element.84.middle_ref, f32[1,1024]{1,0:T(1,128)} %bitcast.126), custom_call_target="tpu_custom_call" | custom-call | flops 4600000000 | tf_op jit(solution)/shard_map/middle_back/pallas_call | solution.py:647
  135.9 1.5 collective-permute-start.12
  137.9 10.4 %collective-permute-done.12.near_ref.refs_3_ = bf16[256,1024]{1,0:T(8,128)(2,1)S(1)} collective-permute-done((bf16[256,1024]{1,0:T(8,128)(2,1)}, bf16[256,1024]{1,0:T(8,128)(2,1)S(1)}, u32[]{:S(2)}, u32[]{:S(2)}) %collective-permute-start.12) | collective-permute-done | bytes 524320 | tf_op jit(solution)/shard_map/ppermute | solution.py:1159
  149.1 6.1 %heads_back.1 = (bf16[2,256,128]{2,1,0:T(8,128)(2,1)}, bf16[2,256,128]{2,1,0:T(8,128)(2,1)}) custom-call(bf16[256,1024]{1,0:T(8,128)(2,1)} %get-tuple-element.94.own_ref.refs_2_, bf16[256,1024]{1,0:T(8,128)(2,1)} %copy-done.29, bf16[2,640,1024]{2,1,0:T(8,128)(2,1)} %get-tuple-element.95.full_ref, bf16[2,256,128]{2,1,0:T(8,128)(2,1)} %get-tuple-element.79.refs_0_.refs_1_, ...), custom_call_target="tpu_custom_call" | custom-call | flops 6899999744 | tf_op jit(solution)/shard_map/heads_back/pallas_call | solution.py:688
  155.2 1.2 collective-permute-start.13
  156.4 6.0 %out_weights.1 = (bf16[4,1120,128]{2,1,0:T(8,128)(2,1)}, bf16[4,1120,128]{2,1,0:T(8,128)(2,1)}) custom-call(s32[2]{0:T(128)} %pad_add_fusion.2.where_ref, bf16[2,256,128]{2,1,0:T(8,128)(2,1)} %get-tuple-element.79.refs_0_.refs_1_, bf16[2,256,128]{2,1,0:T(8,128)(2,1)} %copy-done.8, bf16[256,1024]{1,0:T(8,128)(2,1)} %get-tuple-element.94.own_ref.refs_2_, ...), custom_call_target="tpu_custom_call" | custom-call | flops 5750000128 | tf_op jit(solution)/shard_map/out_weights/pallas_call | solution.py:875
  163.3 1.0 collective-permute-start.14
  164.3 15.0 %attend_back.1 = (bf16[2048,128]{1,0:T(8,128)(2,1)}, f32[2048,128]{1,0:T(8,128)}, bf16[1024,128]{1,0:T(8,128)(2,1)}, bf16[1024,128]{1,0:T(8,128)(2,1)}, f32[2,12...) custom-call(s32[1]{0:T(128)} %bitcast.z_ref, ...), custom_call_target="tpu_custom_call" | custom-call | flops 17250000896 | tf_op jit(solution)/shard_map/attend_back/pallas_call | solution.py:477
  179.3 1.4 collective-permute-start.16
  180.7 2.7 fusion.5
  183.4 3.1 %collective-permute-start.32 = (bf16[1120,128]{1,0:T(8,128)(2,1)}, bf16[1120,128]{1,0:T(8,128)(2,1)}, u32[]{:S(2)}, u32[]{:S(2)}) collective-permute-start(bf16[1120,128]{1,0:T(8,128)(2,1)} %get-tuple-element.182.refs_4_), channel_id=1, source_target_pairs={{0,24},{4,28},{8,16},{12,20},{16,8},{20,12},{24,0},{28,4},{1,25},{... | collective-permute-start | bytes 860168 | tf_op jit(solution)/shard_map/ppermute | solution.py:1159
  188.0 13.3 %weight_grads.1 = (bf16[4,912,128]{2,1,0:T(8,128)(2,1)}, bf16[4,912,128]{2,1,0:T(8,128)(2,1)}, f32[8,1024]{1,0:T(8,128)}) custom-call(s32[2]{0:T(128)} %pad_add_fusion.2.where_ref, bf16[2048,1024]{1,0:T(8,128)(2,1)} %get-tuple-element.97.normed_ref, bf16[2048,128]{1,0:T(8,128)(2,1)} %get-tuple-element.104.key_ref, f32[2048,128]{1,0:T(8,128)} %get-tuple-element.105.value_ref, ...), custom_call_target="tpu_custom_call" | custom-call | flops 17250000896 | tf_op jit(solution)/shard_map/weight_grads/pallas_call | solution.py:1017
  201.3 6.3 %token_parts.1 = (f32[256,1024]{1,0:T(8,128)}, bf16[256,1024]{1,0:T(8,128)(2,1)}) custom-call(bf16[2,3,256,128]{3,2,1,0:T(8,128)(2,1)} %get-tuple-element.113.own_ref, bf16[2,3,256,128]{3,2,1,0:T(8,128)(2,1)} %collective-permute-done.16.far_ref, bf16[1024,1024]{1,0:T(8,128)(2,1)} %get-tuple-element.82.w_ref.w_own_ref, bf16[8,128,1024]{2,1,0:T(8,128)(2,1)} %after.35.w_far_ref), custom_call_target="tpu_custom_call" | custom-call | flops 6899999744 | tf_op jit(solution)/shard_map/token_parts/pallas_call | solution.py:1110
  207.6 2.6 collective-permute-start.21
  210.2 2.1 add_convert_fusion.1
  212.3 1.0 collective-permute-start.20
  213.3 1.1 collective-permute-start.19
  214.4 0.9 collective-permute-start.17
  215.4 1.3 convert_add_fusion.1
  217.4 1.9 slice.175.refs_1_
  220.0 0.9 copy-done.2
  221.7 2.4 collective-permute-start.28
  225.3 1.9 collective-permute-start.22
  227.2 2.1 fusion.10
  229.3 1.3 collective-permute-done.17.near_ref
  230.7 2.5 collective-permute-start.25
  234.8 3.5 %token_sum.1 = f32[256,1024]{1,0:T(8,128)} custom-call(s32[1]{0:T(128)} %bitcast.z_ref, bf16[1024,1024]{1,0:T(8,128)(2,1)} %tok_ref.5, f32[256,1024]{1,0:T(8,128)} %get-tuple-element.112.mid_ref, f32[1,1024]{1,0:T(1,128)} %bitcast.131, f32[256,1024]{1,0:T(8,128)} %get-tuple-element.115.own_ref, bf16[256,1024]{1,0:T(8,128)(2,1)} %collective-permute-done.17.near_ref), custom_call_target="tpu_custom_call" | custom-call | flops 4600000000 | tf_op jit(solution)/shard_map/token_sum/pallas_call | solution.py:1136
  238.6 2.0 collective-permute-done.25.refs_3_
  240.6 3.1 %collective-permute-done.24.refs_2_ = bf16[912,128]{1,0:T(8,128)(2,1)} collective-permute-done((bf16[912,128]{1,0:T(8,128)(2,1)}, bf16[912,128]{1,0:T(8,128)(2,1)}, u32[]{:S(2)}, u32[]{:S(2)}) %collective-permute-start.24) | collective-permute-done | bytes 233504 | tf_op jit(solution)/shard_map/ppermute | solution.py:1159
  243.8 11.0 %collective-permute-done.22.refs_0_ = bf16[128,2048]{1,0:T(8,128)(2,1)} collective-permute-done((bf16[128,2048]{1,0:T(8,128)(2,1)}, bf16[128,2048]{1,0:T(8,128)(2,1)}, u32[]{:S(2)}, u32[]{:S(2)}) %collective-permute-start.22) | collective-permute-done | bytes 524320 | tf_op jit(solution)/shard_map/ppermute | solution.py:1159
  254.9 1.5 fusion.1
  258.4 1.7 fusion.6
  260.1 1.2 convert_add_fusion
  261.3 0.9 slice_bitcast_fusion
  263.0 1.0 copy.81
  (160 shorter events, 23.1 us)
Async XLA Ops:
  7.2 7.1 %copy-start.26 = (s32[1,2048]{1,0:T(1,128)S(1)}, s32[1,2048]{1,0:T(1,128)}, u32[]{:S(2)}) copy-start(s32[1,2048]{1,0:T(1,128)} %param.23) | copy-start | bytes 24580
  7.2 7.1 %copy-start.31 = (f32[1,112]{1,0:T(1,128)S(1)}, f32[1,112]{1,0:T(1,128)}, u32[]{:S(2)}) copy-start(f32[1,112]{1,0:T(1,128)} %param.37) | copy-start | bytes 1348
  7.2 7.6 %copy-start.32 = (f32[1,112]{1,0:T(1,128)S(1)}, f32[1,112]{1,0:T(1,128)}, u32[]{:S(2)}) copy-start(f32[1,112]{1,0:T(1,128)} %param.38) | copy-start | bytes 1348
  7.2 88.0 %all-gather.5.cloned.1.call-start = ((), (), s32[]{:S(2)}) async-start(), calls=%async_computation.2 | async-start | bytes 4718592 | tf_op jit(solution)/shard_map/all_gather | solution.py:1298
  8.2 26.1 %collective-permute-start = (bf16[560,128]{1,0:T(8,128)(2,1)S(1)}, bf16[560,128]{1,0:T(8,128)(2,1)S(1)}, u32[]{:S(2)}, u32[]{:S(2)}) collective-permute-start(bf16[560,128]{1,0:T(8,128)(2,1)S(1)} %dynamic-slice_bitcast_fusion.2), channel_id=1, source_target_pairs={{0,2},{1,3},{2,0},{3,1},{4,6},{5,7},{6,4},{7,5},{8,10},{9,11},{10,... | collective-permute-start | bytes 430088 | tf_op jit(solution)/shard_map/ppermute | solution.py:1159
  14.3 28.5 %collective-permute-start.9 = (bf16[2,128,1024]{2,1,0:T(8,128)(2,1)}, bf16[2,128,1024]{2,1,0:T(8,128)(2,1)S(1)}, u32[]{:S(2)}, u32[]{:S(2)}) collective-permute-start(bf16[2,128,1024]{2,1,0:T(8,128)(2,1)} %pad_maximum_fusion.1), channel_id=1, source_target_pairs={{0,2},{1,3},{2,0},{3,1},{4,6},{5,7},{6,4},{7,5},{8,10},{9,11},{10,... | collective-permute-start | bytes 1572872 | tf_op jit(solution)/shard_map/ppermute | solution.py:1159
  34.3 0.7 copy-start.13
  42.7 0.8 copy-start.5
  43.6 87.7 %all-gather.7.cloned.1.call-start = ((), (), s32[]{:S(2)}) async-start(), calls=%async_computation.3 | async-start | bytes 2359296 | tf_op jit(solution)/shard_map/all_gather | solution.py:1320
  43.7 7.2 %collective-permute-start.4 = (bf16[560,128]{1,0:T(8,128)(2,1)}, bf16[560,128]{1,0:T(8,128)(2,1)S(1)}, u32[]{:S(2)}, u32[]{:S(2)}) collective-permute-start(bf16[560,128]{1,0:T(8,128)(2,1)} %after.22.refs_0_), channel_id=1, source_target_pairs={{0,24},{4,28},{8,16},{12,20},{16,8},{20,12},{24,0},{28,4},{1,25},{... | collective-permute-start | bytes 430088 | tf_op jit(solution)/shard_map/ppermute | solution.py:1159
  46.5 6.7 %collective-permute-start.3 = (bf16[560,128]{1,0:T(8,128)(2,1)}, bf16[560,128]{1,0:T(8,128)(2,1)}, u32[]{:S(2)}, u32[]{:S(2)}) collective-permute-start(bf16[560,128]{1,0:T(8,128)(2,1)} %after.22.refs_0_), channel_id=1, source_target_pairs={{0,16},{4,20},{8,24},{12,28},{16,0},{20,4},{24,8},{28,12},{1,17},{... | collective-permute-start | bytes 430088 | tf_op jit(solution)/shard_map/ppermute | solution.py:1159
  47.0 6.4 %collective-permute-start.2 = (bf16[560,128]{1,0:T(8,128)(2,1)}, bf16[560,128]{1,0:T(8,128)(2,1)}, u32[]{:S(2)}, u32[]{:S(2)}) collective-permute-start(bf16[560,128]{1,0:T(8,128)(2,1)} %after.22.refs_0_), channel_id=1, source_target_pairs={{0,8},{4,12},{8,0},{12,4},{16,24},{20,28},{24,16},{28,20},{1,9},{5... | collective-permute-start | bytes 430088 | tf_op jit(solution)/shard_map/ppermute | solution.py:1159
  47.2 8.8 %copy-start.16 = (bf16[256,1024]{1,0:T(8,128)(2,1)S(1)}, bf16[256,1024]{1,0:T(8,128)(2,1)}, u32[]{:S(2)}) copy-start(bf16[256,1024]{1,0:T(8,128)(2,1)} %cot_ref.3) | copy-start | bytes 1572868
  47.2 8.2 %collective-permute-start.1 = (bf16[2,256,128]{2,1,0:T(8,128)(2,1)}, bf16[2,256,128]{2,1,0:T(8,128)(2,1)S(1)}, u32[]{:S(2)}, u32[]{:S(2)}) collective-permute-start(bf16[2,256,128]{2,1,0:T(8,128)(2,1)} %get-tuple-element.80), channel_id=1, source_target_pairs={{0,2},{1,3},{2,0},{3,1},{4,6},{5,7},{6,4},{7,5},{8,10},{9,11},{10,... | collective-permute-start | bytes 393224 | tf_op jit(solution)/shard_map/ppermute | solution.py:1159
  50.8 2.5 copy-start.30
  55.4 0.7 copy-start.8
  56.0 3.1 %collective-permute-start.5 = (bf16[4,560,128]{2,1,0:T(8,128)(2,1)}, bf16[4,560,128]{2,1,0:T(8,128)(2,1)}, u32[]{:S(2)}, u32[]{:S(2)}) collective-permute-start(bf16[4,560,128]{2,1,0:T(8,128)(2,1)} %after.23.refs_3_), channel_id=1, source_target_pairs={{0,4},{4,0},{8,12},{12,8},{16,20},{20,16},{24,28},{28,24},{1,5},{5... | collective-permute-start | bytes 1720328 | tf_op jit(solution)/shard_map/ppermute | solution.py:1159
  57.5 30.6 %collective-permute-start.7 = (bf16[256,1024]{1,0:T(8,128)(2,1)}, bf16[256,1024]{1,0:T(8,128)(2,1)S(1)}, u32[]{:S(2)}, u32[]{:S(2)}) collective-permute-start(bf16[256,1024]{1,0:T(8,128)(2,1)} %after.25), channel_id=1, source_target_pairs={{0,1},{1,0},{2,3},{3,2},{4,5},{5,4},{6,7},{7,6},{8,9},{9,8},{10,11... | collective-permute-start | bytes 1572872 | tf_op jit(solution)/shard_map/ppermute | solution.py:1159
  65.5 23.5 %collective-permute-start.8 = (bf16[256,1024]{1,0:T(8,128)(2,1)}, bf16[256,1024]{1,0:T(8,128)(2,1)}, u32[]{:S(2)}, u32[]{:S(2)}) collective-permute-start(bf16[256,1024]{1,0:T(8,128)(2,1)} %get-tuple-element.83), channel_id=1, source_target_pairs={{0,1},{1,0},{2,3},{3,2},{4,5},{5,4},{6,7},{7,6},{8,9},{9,8},{10,11... | collective-permute-start | bytes 1572872 | tf_op jit(solution)/shard_map/ppermute | solution.py:1159
  68.1 20.0 %collective-permute-start.6 = (bf16[128,1024]{1,0:T(8,128)(2,1)}, bf16[128,1024]{1,0:T(8,128)(2,1)S(1)}, u32[]{:S(2)}, u32[]{:S(2)}) collective-permute-start(bf16[128,1024]{1,0:T(8,128)(2,1)} %after.24), channel_id=1, source_target_pairs={{0,2},{1,3},{2,0},{3,1},{4,6},{5,7},{6,4},{7,5},{8,10},{9,11},{10,... | collective-permute-start | bytes 786440 | tf_op jit(solution)/shard_map/ppermute | solution.py:1159
  88.1 0.7 copy-start.4
  88.1 0.9 copy-start.17
  91.6 125.9 %reduce-scatter.2.cloned.1.call-start = ((), (), s32[]{:S(2)}) async-start(), calls=%async_computation.1 | async-start | bytes 9437184 | tf_op jit(solution)/shard_map/reduce_scatter | solution.py:1328
  91.8 15.5 %collective-permute-start.10 = (bf16[256,1024]{1,0:T(8,128)(2,1)}, bf16[256,1024]{1,0:T(8,128)(2,1)S(1)}, u32[]{:S(2)}, u32[]{:S(2)}) collective-permute-start(bf16[256,1024]{1,0:T(8,128)(2,1)} %get-tuple-element.85.up_ref.refs_0_.refs_1_), channel_id=1, source_target_pairs={{0,1},{1,0},{2,3},{3,2},{4,5},{5,4},{6,7},{7,6},{8,9},{9,8},{10,11... | collective-permute-start | bytes 1572872 | tf_op jit(solution)/shard_map/ppermute | solution.py:1159
  107.3 0.8 copy-start.28
  118.2 13.3 %collective-permute-start.11 = (bf16[256,1024]{1,0:T(8,128)(2,1)}, bf16[256,1024]{1,0:T(8,128)(2,1)S(1)}, u32[]{:S(2)}, u32[]{:S(2)}) collective-permute-start(bf16[256,1024]{1,0:T(8,128)(2,1)} %get-tuple-element.93), channel_id=1, source_target_pairs={{0,1},{1,0},{2,3},{3,2},{4,5},{5,4},{6,7},{7,6},{8,9},{9,8},{10,11... | collective-permute-start | bytes 1572872 | tf_op jit(solution)/shard_map/ppermute | solution.py:1159
  131.5 0.8 copy-start.15
  135.9 12.4 %collective-permute-start.12 = (bf16[256,1024]{1,0:T(8,128)(2,1)}, bf16[256,1024]{1,0:T(8,128)(2,1)S(1)}, u32[]{:S(2)}, u32[]{:S(2)}) collective-permute-start(bf16[256,1024]{1,0:T(8,128)(2,1)} %get-tuple-element.94.own_ref.refs_2_), channel_id=1, source_target_pairs={{0,1},{1,0},{2,3},{3,2},{4,5},{5,4},{6,7},{7,6},{8,9},{9,8},{10,11... | collective-permute-start | bytes 1572872 | tf_op jit(solution)/shard_map/ppermute | solution.py:1159
  148.3 0.8 copy-start.29
  155.2 7.5 %collective-permute-start.13 = (bf16[2,256,128]{2,1,0:T(8,128)(2,1)}, bf16[2,256,128]{2,1,0:T(8,128)(2,1)S(1)}, u32[]{:S(2)}, u32[]{:S(2)}) collective-permute-start(bf16[2,256,128]{2,1,0:T(8,128)(2,1)} %get-tuple-element.96), channel_id=1, source_target_pairs={{0,2},{1,3},{2,0},{3,1},{4,6},{5,7},{6,4},{7,5},{8,10},{9,11},{10,... | collective-permute-start | bytes 393224 | tf_op jit(solution)/shard_map/ppermute | solution.py:1159
  162.4 18.4 %collective-permute-start.15 = (bf16[4,1120,128]{2,1,0:T(8,128)(2,1)}, bf16[4,1120,128]{2,1,0:T(8,128)(2,1)}, u32[]{:S(2)}, u32[]{:S(2)}) collective-permute-start(bf16[4,1120,128]{2,1,0:T(8,128)(2,1)} %get-tuple-element.108), channel_id=1, source_target_pairs={{0,4},{4,0},{8,12},{12,8},{16,20},{20,16},{24,28},{28,24},{1,5},{5... | collective-permute-start | bytes 3440648 | tf_op jit(solution)/shard_map/ppermute | solution.py:1159
  163.3 23.9 %collective-permute-start.14 = (bf16[256,1024]{1,0:T(8,128)(2,1)}, bf16[256,1024]{1,0:T(8,128)(2,1)S(1)}, u32[]{:S(2)}, u32[]{:S(2)}) collective-permute-start(bf16[256,1024]{1,0:T(8,128)(2,1)} %after.31), channel_id=1, source_target_pairs={{0,1},{1,0},{2,3},{3,2},{4,5},{5,4},{6,7},{7,6},{8,9},{9,8},{10,11... | collective-permute-start | bytes 1572872 | tf_op jit(solution)/shard_map/ppermute | solution.py:1159
  179.3 21.9 %collective-permute-start.16 = (bf16[2,3,256,128]{3,2,1,0:T(8,128)(2,1)}, bf16[2,3,256,128]{3,2,1,0:T(8,128)(2,1)}, u32[]{:S(2)}, u32[]{:S(2)}) collective-permute-start(bf16[2,3,256,128]{3,2,1,0:T(8,128)(2,1)} %get-tuple-element.114), channel_id=1, source_target_pairs={{0,2},{1,3},{2,0},{3,1},{4,6},{5,7},{6,4},{7,5},{8,10},{9,11},{10,... | collective-permute-start | bytes 1179656 | tf_op jit(solution)/shard_map/ppermute | solution.py:1159
  183.4 3.8 %copy-start.9 = (bf16[1120,128]{1,0:T(8,128)(2,1)}, bf16[1120,128]{1,0:T(8,128)(2,1)S(1)}, u32[]{:S(2)}) copy-start(bf16[1120,128]{1,0:T(8,128)(2,1)S(1)} %get-tuple-element.184.refs_2_) | copy-start | bytes 860164
  183.4 28.9 %collective-permute-start.32 = (bf16[1120,128]{1,0:T(8,128)(2,1)}, bf16[1120,128]{1,0:T(8,128)(2,1)}, u32[]{:S(2)}, u32[]{:S(2)}) collective-permute-start(bf16[1120,128]{1,0:T(8,128)(2,1)} %get-tuple-element.182.refs_4_), channel_id=1, source_target_pairs={{0,24},{4,28},{8,16},{12,20},{16,8},{20,12},{24,0},{28,4},{1,25},{... | collective-permute-start | bytes 860168 | tf_op jit(solution)/shard_map/ppermute | solution.py:1159
  186.6 26.8 %collective-permute-start.31 = (bf16[1120,128]{1,0:T(8,128)(2,1)}, bf16[1120,128]{1,0:T(8,128)(2,1)}, u32[]{:S(2)}, u32[]{:S(2)}) collective-permute-start(bf16[1120,128]{1,0:T(8,128)(2,1)} %get-tuple-element.183.refs_3_), channel_id=1, source_target_pairs={{0,16},{4,20},{8,24},{12,28},{16,0},{20,4},{24,8},{28,12},{1,17},{... | collective-permute-start | bytes 860168 | tf_op jit(solution)/shard_map/ppermute | solution.py:1159
  186.6 27.9 %collective-permute-start.30 = (bf16[1120,128]{1,0:T(8,128)(2,1)S(1)}, bf16[1120,128]{1,0:T(8,128)(2,1)}, u32[]{:S(2)}, u32[]{:S(2)}) collective-permute-start(bf16[1120,128]{1,0:T(8,128)(2,1)S(1)} %get-tuple-element.184.refs_2_), channel_id=1, source_target_pairs={{0,8},{4,12},{8,0},{12,4},{16,24},{20,28},{24,16},{28,20},{1,9},{5... | collective-permute-start | bytes 860168 | tf_op jit(solution)/shard_map/ppermute | solution.py:1159
  187.2 0.8 copy-start.1
  207.6 11.8 %collective-permute-start.18 = (bf16[4,912,128]{2,1,0:T(8,128)(2,1)}, bf16[4,912,128]{2,1,0:T(8,128)(2,1)S(1)}, u32[]{:S(2)}, u32[]{:S(2)}) collective-permute-start(bf16[4,912,128]{2,1,0:T(8,128)(2,1)} %after.37.refs_1_), channel_id=1, source_target_pairs={{0,4},{4,0},{8,12},{12,8},{16,20},{20,16},{24,28},{28,24},{1,5},{5... | collective-permute-start | bytes 2801672 | tf_op jit(solution)/shard_map/ppermute | solution.py:1159
  207.6 2.6 copy-start.11
  207.6 2.6 copy-start.10
  207.6 11.7 %collective-permute-start.21 = (f32[8,1024]{1,0:T(8,128)}, f32[8,1024]{1,0:T(8,128)S(1)}, u32[]{:S(2)}, u32[]{:S(2)}) collective-permute-start(f32[8,1024]{1,0:T(8,128)} %after.36), channel_id=1, source_target_pairs={{0,3},{1,2},{2,1},{3,0},{4,7},{5,6},{6,5},{7,4},{8,11},{9,10},{10,... | collective-permute-start | bytes 98312 | tf_op jit(solution)/shard_map/ppermute | solution.py:1159
  212.3 2.2 copy-start.27
  212.3 3.1 %copy-start.3 = (bf16[1120,128]{1,0:T(8,128)(2,1)S(1)}, bf16[1120,128]{1,0:T(8,128)(2,1)}, u32[]{:S(2)}) copy-start(bf16[1120,128]{1,0:T(8,128)(2,1)} %get-tuple-element.185.refs_1_) | copy-start | bytes 860164
  212.3 7.1 %collective-permute-start.20 = (f32[8,1024]{1,0:T(8,128)}, f32[8,1024]{1,0:T(8,128)S(1)}, u32[]{:S(2)}, u32[]{:S(2)}) collective-permute-start(f32[8,1024]{1,0:T(8,128)} %after.36), channel_id=1, source_target_pairs={{0,2},{1,3},{2,0},{3,1},{4,6},{5,7},{6,4},{7,5},{8,10},{9,11},{10,... | collective-permute-start | bytes 98312 | tf_op jit(solution)/shard_map/ppermute | solution.py:1159
  213.3 6.0 %collective-permute-start.19 = (f32[8,1024]{1,0:T(8,128)}, f32[8,1024]{1,0:T(8,128)S(1)}, u32[]{:S(2)}, u32[]{:S(2)}) collective-permute-start(f32[8,1024]{1,0:T(8,128)} %after.36), channel_id=1, source_target_pairs={{0,1},{1,0},{2,3},{3,2},{4,5},{5,4},{6,7},{7,6},{8,9},{9,8},{10,11... | collective-permute-start | bytes 98312 | tf_op jit(solution)/shard_map/ppermute | solution.py:1159
  214.4 16.2 %collective-permute-start.17 = (bf16[256,1024]{1,0:T(8,128)(2,1)S(1)}, bf16[256,1024]{1,0:T(8,128)(2,1)}, u32[]{:S(2)}, u32[]{:S(2)}) collective-permute-start(bf16[256,1024]{1,0:T(8,128)(2,1)S(1)} %copy-done.27), channel_id=1, source_target_pairs={{0,1},{1,0},{2,3},{3,2},{4,5},{5,4},{6,7},{7,6},{8,9},{9,8},{10,11... | collective-permute-start | bytes 1572872 | tf_op jit(solution)/shard_map/ppermute | solution.py:1159
  215.4 11.9 %copy-start = (bf16[4,912,128]{2,1,0:T(8,128)(2,1)S(1)}, bf16[4,912,128]{2,1,0:T(8,128)(2,1)}, u32[]{:S(2)}) copy-start(bf16[4,912,128]{2,1,0:T(8,128)(2,1)} %get-tuple-element.111.refs_1_) | copy-start | bytes 2801668
  216.7 12.6 %copy-start.6 = (f32[1120,128]{1,0:T(8,128)}, f32[1120,128]{1,0:T(8,128)S(1)}, u32[]{:S(2)}) copy-start(f32[1120,128]{1,0:T(8,128)S(1)} %convert_add_fusion.1) | copy-start | bytes 1720324
  220.0 0.9 copy-start.2
  221.7 11.5 %collective-permute-start.28 = (f32[8,1024]{1,0:T(8,128)S(1)}, f32[8,1024]{1,0:T(8,128)S(1)}, u32[]{:S(2)}, u32[]{:S(2)}) collective-permute-start(f32[8,1024]{1,0:T(8,128)S(1)} %add_add_fusion.1), channel_id=1, source_target_pairs={{0,24},{4,28},{8,16},{12,20},{16,8},{20,12},{24,0},{28,4},{1,25},{... | collective-permute-start | bytes 98312 | tf_op jit(solution)/shard_map/ppermute | solution.py:1159
  224.2 9.6 %collective-permute-start.27 = (f32[8,1024]{1,0:T(8,128)S(1)}, f32[8,1024]{1,0:T(8,128)S(1)}, u32[]{:S(2)}, u32[]{:S(2)}) collective-permute-start(f32[8,1024]{1,0:T(8,128)S(1)} %add_add_fusion.1), channel_id=1, source_target_pairs={{0,16},{4,20},{8,24},{12,28},{16,0},{20,4},{24,8},{28,12},{1,17},{... | collective-permute-start | bytes 98312 | tf_op jit(solution)/shard_map/ppermute | solution.py:1159
  224.7 13.6 %collective-permute-start.26 = (f32[8,1024]{1,0:T(8,128)S(1)}, f32[8,1024]{1,0:T(8,128)}, u32[]{:S(2)}, u32[]{:S(2)}) collective-permute-start(f32[8,1024]{1,0:T(8,128)S(1)} %add_add_fusion.1), channel_id=1, source_target_pairs={{0,8},{4,12},{8,0},{12,4},{16,24},{20,28},{24,16},{28,20},{1,9},{5... | collective-permute-start | bytes 98312 | tf_op jit(solution)/shard_map/ppermute | solution.py:1159
  225.3 29.6 %collective-permute-start.22 = (bf16[128,2048]{1,0:T(8,128)(2,1)}, bf16[128,2048]{1,0:T(8,128)(2,1)}, u32[]{:S(2)}, u32[]{:S(2)}) collective-permute-start(bf16[128,2048]{1,0:T(8,128)(2,1)} %get-tuple-element.122), channel_id=1, source_target_pairs={{0,2},{1,3},{2,0},{3,1},{4,6},{5,7},{6,4},{7,5},{8,10},{9,11},{10,... | collective-permute-start | bytes 1572872 | tf_op jit(solution)/shard_map/ppermute | solution.py:1159
  230.7 9.9 %collective-permute-start.25 = (bf16[912,128]{1,0:T(8,128)(2,1)}, bf16[912,128]{1,0:T(8,128)(2,1)}, u32[]{:S(2)}, u32[]{:S(2)}) collective-permute-start(bf16[912,128]{1,0:T(8,128)(2,1)} %get-tuple-element.186), channel_id=1, source_target_pairs={{0,24},{4,28},{8,16},{12,20},{16,8},{20,12},{24,0},{28,4},{1,25},{... | collective-permute-start | bytes 700424 | tf_op jit(solution)/shard_map/ppermute | solution.py:1159
  233.2 10.5 %collective-permute-start.24 = (bf16[912,128]{1,0:T(8,128)(2,1)}, bf16[912,128]{1,0:T(8,128)(2,1)}, u32[]{:S(2)}, u32[]{:S(2)}) collective-permute-start(bf16[912,128]{1,0:T(8,128)(2,1)} %get-tuple-element.187), channel_id=1, source_target_pairs={{0,16},{4,20},{8,24},{12,28},{16,0},{20,4},{24,8},{28,12},{1,17},{... | collective-permute-start | bytes 700424 | tf_op jit(solution)/shard_map/ppermute | solution.py:1159
  234.4 9.4 %collective-permute-start.23 = (bf16[912,128]{1,0:T(8,128)(2,1)}, bf16[912,128]{1,0:T(8,128)(2,1)}, u32[]{:S(2)}, u32[]{:S(2)}) collective-permute-start(bf16[912,128]{1,0:T(8,128)(2,1)} %get-tuple-element.188), channel_id=1, source_target_pairs={{0,8},{4,12},{8,0},{12,4},{16,24},{20,28},{24,16},{28,20},{1,9},{5... | collective-permute-start | bytes 700424 | tf_op jit(solution)/shard_map/ppermute | solution.py:1159
  238.4 19.4 %collective-permute-start.33 = (bf16[560,128]{1,0:T(8,128)(2,1)}, bf16[560,128]{1,0:T(8,128)(2,1)S(1)}, u32[]{:S(2)}, u32[]{:S(2)}) collective-permute-start(bf16[560,128]{1,0:T(8,128)(2,1)} %slice.225), channel_id=1, source_target_pairs={{0,2},{1,3},{2,0},{3,1},{4,6},{5,7},{6,4},{7,5},{8,10},{9,11},{10,... | collective-permute-start | bytes 430088 | tf_op jit(solution)/shard_map/ppermute | solution.py:1159
  254.9 3.6 %copy-start.7 = (f32[1120,128]{1,0:T(8,128)S(1)}, f32[1120,128]{1,0:T(8,128)}, u32[]{:S(2)}) copy-start(f32[1120,128]{1,0:T(8,128)} %copy-done.6) | copy-start | bytes 1720324
  256.4 3.7 %copy-start.12 = (bf16[128,4096]{1,0:T(8,128)(2,1)S(1)}, bf16[128,4096]{1,0:T(8,128)(2,1)}, u32[]{:S(2)}) copy-start(bf16[128,4096]{1,0:T(8,128)(2,1)} %reduce-scatter.2.cloned.1.call-done) | copy-start | bytes 3145732
  257.8 0.7 copy-start.14
  260.1 2.1 copy-start.20
  260.1 2.1 copy-start.22
  262.9 2.2 collective-permute-start.29
  (6 other events, 3.7 us)
Sparse Core Ops, SparseCore 0:
  43.7 38.2 all-gather.4
  91.7 28.8 all-gather.6
  132.5 79.9 reduce-scatter.1
where the time goes:
time: 274 us; the launch traced here: 273 us
  Pallas kernels  116 us (42%)
  waiting for transfers between devices  50.9 us (19%)
  starting transfers between devices  45 us (16%)
  local copies, waits for them, and re-layouts  25.3 us (9%)
  other arithmetic  19.1 us (7%)
  between operations  14.1 us (5%)
  matrix products  3 us (1%)
    ppermute x34, waiting for transfers between devices, swap(): return lax.ppermute(array, axis, [(i, i ^ mask) for i in range(size)])  50.8 us
    ppermute x34, starting transfers between devices, swap(): return lax.ppermute(array, axis, [(i, i ^ mask) for i in range(size)])  44.7 us
    pallas_call x2, Pallas kernels, feed(): pl.pallas_call(functools.partial(feed_kernel, half), grid=(2 * half,), in...  20.6 us
    pallas_call x1, Pallas kernels, attend_back(): pl.pallas_call(functools.partial(attend_back_kernel, span, experts, head_...  15 us
    pallas_call x1, Pallas kernels, weight_grads(): pl.pallas_call(functools.partial(weights_kernel, experts, head_dim, count...  13.3 us
    unnamed x70, local copies, waits for them, and re-layouts  12.8 us
    pallas_call x1, Pallas kernels, project(): pl.pallas_call(functools.partial(project_kernel, experts, head_dim, mem_s...  11.4 us
    pallas_call x1, Pallas kernels, feed_weights(): pl.pallas_call(functools.partial(feed_weights_kernel, count, half), grid=...  11.2 us
  transfers between devices with their start and end apart: 37, of which 13 were waited for; matrix products, arithmetic and copies ran while one was open for 11% of the time, Pallas kernels for 42%

commit v1 on v0

--- a/solution.py
+++ b/solution.py
@@ -290,7 +290,8 @@
         reverse = mm_nt(qp_ref[rows, :], rel_ref[...])
         reverse = jnp.concatenate([reverse, jnp.zeros((ROWS, ROWS), F32)], axis=1)
         scores = content + pltpu.roll(reverse, 1, 1, stride=1, stride_axis=0)
-        same = segk_ref[b] == segq_ref[rows, :]
+        own = jnp.concatenate([segq_ref[:, rows], jnp.zeros((7, ROWS), jnp.int32)], axis=0)
+        same = segk_ref[b].astype(F32) == own.astype(F32).T[:, 0:1]
         allowed = jnp.concatenate([same[:, :span], same[:, span:] & causal], axis=1)
         scores = jnp.where(allowed, scores, -1e30)
         expo = jnp.exp(scores - jnp.max(scores, axis=1, keepdims=True))
@@ -328,7 +329,7 @@
                 whole(keys, LANES),
                 whole(span, LANES),
                 pl.BlockSpec((count, 1, wide), lambda i, z: (i, 0, 0)),
-                pl.BlockSpec((big, 1), row),
+                pl.BlockSpec((1, big), lambda i, z: (0, i)),
                 pl.BlockSpec((big, LANES), row),
             ],
             out_specs=[
@@ -1282,7 +1283,7 @@
         value_vecs,
         rel_reverse,
         seg_keys,
-        seg[mem_len:, None],
+        seg[None, mem_len:],
         ogate,
         head_dim,
     )

time: 274 us -> 274 us (level)
  no operation moved by 1% of the time
where the time goes in v1:
time: 274 us; the launch traced here: 273 us
  Pallas kernels  116 us (42%)
  waiting for transfers between devices  50.8 us (19%)
  starting transfers between devices  45 us (16%)
  local copies, waits for them, and re-layouts  24.9 us (9%)
  other arithmetic  19.1 us (7%)
  between operations  14.1 us (5%)
  matrix products  3 us (1%)
    ppermute x34, waiting for transfers between devices, swap(): return lax.ppermute(array, axis, [(i, i ^ mask) for i in range(size)])  50.8 us
    ppermute x34, starting transfers between devices, swap(): return lax.ppermute(array, axis, [(i, i ^ mask) for i in range(size)])  44.7 us
    pallas_call x2, Pallas kernels, feed(): pl.pallas_call(functools.partial(feed_kernel, half), grid=(2 * half,), in...  20.6 us
    pallas_call x1, Pallas kernels, attend_back(): pl.pallas_call(functools.partial(attend_back_kernel, span, experts, head_...  15 us
    pallas_call x1, Pallas kernels, weight_grads(): pl.pallas_call(functools.partial(weights_kernel, experts, head_dim, count...  13.3 us
    unnamed x70, local copies, waits for them, and re-layouts  12.8 us
    pallas_call x1, Pallas kernels, project(): pl.pallas_call(functools.partial(project_kernel, experts, head_dim, mem_s...  11.4 us
    pallas_call x1, Pallas kernels, feed_weights(): pl.pallas_call(functools.partial(feed_weights_kernel, count, half), grid=...  11.2 us
  transfers between devices with their start and end apart: 37, of which 13 were waited for; matrix products, arithmetic and copies ran while one was open for 11% of the time, Pallas kernels for 42%

profile of v1, /device:TPU:0, one launch (start us, length us, event | category | flops | bytes accessed | tf_op | source)
XLA Modules:
  0.0 272.7 jit_solution(17759691823556478315)
XLA Ops:
  7.3 0.9 dynamic-slice_bitcast_fusion.2
  8.2 4.1 %collective-permute-start = (bf16[560,128]{1,0:T(8,128)(2,1)S(1)}, bf16[560,128]{1,0:T(8,128)(2,1)S(1)}, u32[]{:S(2)}, u32[]{:S(2)}) collective-permute-start(bf16[560,128]{1,0:T(8,128)(2,1)S(1)} %dynamic-slice_bitcast_fusion.2), channel_id=1, source_target_pairs={{0,2},{1,3},{2,0},{3,1},{4,6},{5,7},{6,4},{7,5},{8,10},{9,11},{10,... | collective-permute-start | bytes 430088 | tf_op jit(solution)/shard_map/ppermute | solution.py:1160
  12.3 1.1 dynamic-slice_bitcast_fusion
  13.4 0.9 pad_maximum_fusion.1
  17.8 1.6 pad_maximum_fusion.table_ref
  19.5 11.4 %project.1 = (bf16[1024,1024]{1,0:T(8,128)(2,1)}, bf16[2048,1024]{1,0:T(8,128)(2,1)}, bf16[2048,128]{1,0:T(8,128)(2,1)}, bf16[2048,128]{1,0:T(8,128)(2,1)}, bf16...) custom-call(bf16[1024,1024]{1,0:T(8,128)(2,1)} %bitcast.114, ...), custom_call_target="tpu_custom_call" | custom-call | flops 13799999488 | tf_op jit(solution)/shard_map/project/pallas_call | solution.py:220
  30.9 3.0 %convolution_convert_fusion.rel_ref = bf16[1024,128]{1,0:T(8,128)(2,1)} fusion(bf16[1024,1024]{1,0:T(8,128)(2,1)} %pad_maximum_fusion.table_ref, bf16[112,1024]{1,0:T(8,128)(2,1)} %bitcast.104), kind=kOutput, calls=%fused_computation.3 | convolution fusion | flops 268566528 | bytes 2588672 | tf_op jit(solution)/shard_map/dot_general | solution.py:26
  34.5 7.9 %attend.1 = (f32[1024,128]{1,0:T(8,128)}, bf16[1024,1280]{1,0:T(8,128)(2,1)}, bf16[2,256,128]{2,1,0:T(8,128)(2,1)}, bf16[2,256,128]{2,1,0:T(8,128)(2,1)}) custom-call(s32[1]{0:T(128)} %bitcast.z_ref, bf16[1024,128]{1,0:T(8,128)(2,1)} %get-tuple-element.74.qc_ref.refs_1_, bf16[1024,128]{1,0:T(8,128)(2,1)} %get-tuple-element.75.qp_ref, ...), custom_call_target="tpu_custom_call" | custom-call | flops 9200000000 | tf_op jit(solution)/shard_map/attend/pallas_call | solution.py:320
  42.4 0.8 copy-done.5
  43.4 2.8 %collective-permute-start.4 = (bf16[560,128]{1,0:T(8,128)(2,1)}, bf16[560,128]{1,0:T(8,128)(2,1)S(1)}, u32[]{:S(2)}, u32[]{:S(2)}) collective-permute-start(bf16[560,128]{1,0:T(8,128)(2,1)} %after.22.refs_0_), channel_id=1, source_target_pairs={{0,24},{4,28},{8,16},{12,20},{16,8},{20,12},{24,0},{28,4},{1,25},{... | collective-permute-start | bytes 430088 | tf_op jit(solution)/shard_map/ppermute | solution.py:1160
  46.9 2.9 %collective-permute-start.1 = (bf16[2,256,128]{2,1,0:T(8,128)(2,1)}, bf16[2,256,128]{2,1,0:T(8,128)(2,1)S(1)}, u32[]{:S(2)}, u32[]{:S(2)}) collective-permute-start(bf16[2,256,128]{2,1,0:T(8,128)(2,1)} %get-tuple-element.80), channel_id=1, source_target_pairs={{0,2},{1,3},{2,0},{3,1},{4,6},{5,7},{6,4},{7,5},{8,10},{9,11},{10,... | collective-permute-start | bytes 393224 | tf_op jit(solution)/shard_map/ppermute | solution.py:1160
  50.5 2.4 collective-permute-done.3.refs_2_
  53.0 2.1 pile.1.refs_0_
  55.8 0.8 copy.81.refs_0_
  57.2 1.6 collective-permute-start.7
  58.8 6.4 %mix.1 = (bf16[2,640,1024]{2,1,0:T(8,128)(2,1)}, f32[256,1024]{1,0:T(8,128)}, bf16[256,1024]{1,0:T(8,128)(2,1)}) custom-call(s32[3]{0:T(128)} %pad_add_fusion.1.where_ref, bf16[2,256,128]{2,1,0:T(8,128)(2,1)} %get-tuple-element.79.refs_0_.refs_1_, bf16[2,256,128]{2,1,0:T(8,128)(2,1)} %copy-done.8, bf16[560,1024]{1,0:T(8,128)(2,1)} %bitcast.105, ...), custom_call_target="tpu_custom_call" | custom-call | flops 8049999872 | tf_op jit(solution)/shard_map/mix/pallas_call | solution.py:566
  65.2 0.9 collective-permute-start.8
  66.1 1.7 constant_dynamic-slice_fusion.refs_0_
  67.8 2.6 collective-permute-start.6
  70.4 17.4 %collective-permute-done.6.refs_1_.refs_0_ = bf16[128,1024]{1,0:T(8,128)(2,1)S(1)} collective-permute-done((bf16[128,1024]{1,0:T(8,128)(2,1)}, bf16[128,1024]{1,0:T(8,128)(2,1)S(1)}, u32[]{:S(2)}, u32[]{:S(2)}) %collective-permute-start.6) | collective-permute-done | bytes 262176 | tf_op jit(solution)/shard_map/ppermute | solution.py:1160
  88.7 2.5 middle.1
  91.5 3.5 %collective-permute-start.10 = (bf16[256,1024]{1,0:T(8,128)(2,1)}, bf16[256,1024]{1,0:T(8,128)(2,1)S(1)}, u32[]{:S(2)}, u32[]{:S(2)}) collective-permute-start(bf16[256,1024]{1,0:T(8,128)(2,1)} %get-tuple-element.85.up_ref.refs_0_.refs_1_), channel_id=1, source_target_pairs={{0,1},{1,0},{2,3},{3,2},{4,5},{5,4},{6,7},{7,6},{8,9},{9,8},{10,11... | collective-permute-start | bytes 1572872 | tf_op jit(solution)/shard_map/ppermute | solution.py:1160
  95.0 10.4 %feed.2 = (bf16[256,2048]{1,0:T(8,128)(2,1)}, bf16[256,2048]{1,0:T(8,128)(2,1)}, f32[256,1024]{1,0:T(8,128)}, f32[256,1024]{1,0:T(8,128)}) custom-call(bf16[256,1024]{1,0:T(8,128)(2,1)} %get-tuple-element.85.up_ref.refs_0_.refs_1_, bf16[256,1024]{1,0:T(8,128)(2,1)} %cot_ref.3, bf16[1024,1024]{1,0:T(8,128)(2,1)} %wu_ref.3, bf16[1024,1024]{1,0:T(8,128)(2,1)} %wd_ref.3, ...), custom_call_target="tpu_custom_call" | custom-call | flops 11500000256 | tf_op jit(solution)/shard_map/feed/pallas_call | solution.py:762
  105.4 1.6 collective-permute-done.10.up_ref.refs_1_
  107.0 0.8 copy-done.28
  107.8 10.1 %feed.3 = (bf16[256,2048]{1,0:T(8,128)(2,1)}, bf16[256,2048]{1,0:T(8,128)(2,1)}, bf16[256,1024]{1,0:T(8,128)(2,1)}, bf16[256,1024]{1,0:T(8,128)(2,1)}) custom-call(bf16[256,1024]{1,0:T(8,128)(2,1)} %copy-done.28, bf16[256,1024]{1,0:T(8,128)(2,1)} %copy-done.17, bf16[1024,1024]{1,0:T(8,128)(2,1)} %wu_ref.3, bf16[1024,1024]{1,0:T(8,128)(2,1)} %wd_ref.3, ...), custom_call_target="tpu_custom_call" | custom-call | flops 11500000256 | tf_op jit(solution)/shard_map/feed/pallas_call | solution.py:762
  118.0 1.8 collective-permute-start.11
  119.8 11.2 %feed_weights.1.refs_0_ = bf16[1024,4096]{1,0:T(8,128)(2,1)} custom-call(bf16[256,1024]{1,0:T(8,128)(2,1)} %get-tuple-element.85.up_ref.refs_0_.refs_1_, bf16[256,1024]{1,0:T(8,128)(2,1)} %copy-done.28, bf16[256,1024]{1,0:T(8,128)(2,1)} %cot_ref.3, bf16[256,1024]{1,0:T(8,128)(2,1)} %copy-done.17, bf16[256,2048]{1,0:T(8,128)(2,1)} %get-tuple-element.87.refs_0_.refs_4_, ...), custom_call_target="tpu_custom_call" | custom-call | flops 12650000384 | tf_op jit(solution)/shard_map/feed_weights/pallas_call | solution.py:823
  131.2 0.8 copy-done.15
  132.1 3.5 %middle_back.1 = (f32[256,1024]{1,0:T(8,128)}, bf16[256,1024]{1,0:T(8,128)(2,1)}, f32[2,1024]{1,0:T(2,128)}) custom-call(f32[256,1024]{1,0:T(8,128)} %after.30.own_ref, bf16[256,1024]{1,0:T(8,128)(2,1)} %copy-done.15, bf16[256,1024]{1,0:T(8,128)(2,1)} %cot_ref.3, f32[256,1024]{1,0:T(8,128)} %get-tuple-element.84.middle_ref, f32[1,1024]{1,0:T(1,128)} %bitcast.124), custom_call_target="tpu_custom_call" | custom-call | flops 4600000000 | tf_op jit(solution)/shard_map/middle_back/pallas_call | solution.py:648
  135.6 1.5 collective-permute-start.12
  137.6 10.4 %collective-permute-done.12.near_ref.refs_3_ = bf16[256,1024]{1,0:T(8,128)(2,1)S(1)} collective-permute-done((bf16[256,1024]{1,0:T(8,128)(2,1)}, bf16[256,1024]{1,0:T(8,128)(2,1)S(1)}, u32[]{:S(2)}, u32[]{:S(2)}) %collective-permute-start.12) | collective-permute-done | bytes 524320 | tf_op jit(solution)/shard_map/ppermute | solution.py:1160
  148.8 6.1 %heads_back.1 = (bf16[2,256,128]{2,1,0:T(8,128)(2,1)}, bf16[2,256,128]{2,1,0:T(8,128)(2,1)}) custom-call(bf16[256,1024]{1,0:T(8,128)(2,1)} %get-tuple-element.94.own_ref.refs_2_, bf16[256,1024]{1,0:T(8,128)(2,1)} %copy-done.29, bf16[2,640,1024]{2,1,0:T(8,128)(2,1)} %get-tuple-element.95.full_ref, bf16[2,256,128]{2,1,0:T(8,128)(2,1)} %get-tuple-element.79.refs_0_.refs_1_, ...), custom_call_target="tpu_custom_call" | custom-call | flops 6899999744 | tf_op jit(solution)/shard_map/heads_back/pallas_call | solution.py:689
  154.9 1.2 collective-permute-start.13
  156.1 6.0 %out_weights.1 = (bf16[4,1120,128]{2,1,0:T(8,128)(2,1)}, bf16[4,1120,128]{2,1,0:T(8,128)(2,1)}) custom-call(s32[2]{0:T(128)} %pad_add_fusion.2.where_ref, bf16[2,256,128]{2,1,0:T(8,128)(2,1)} %get-tuple-element.79.refs_0_.refs_1_, bf16[2,256,128]{2,1,0:T(8,128)(2,1)} %copy-done.8, bf16[256,1024]{1,0:T(8,128)(2,1)} %get-tuple-element.94.own_ref.refs_2_, ...), custom_call_target="tpu_custom_call" | custom-call | flops 5750000128 | tf_op jit(solution)/shard_map/out_weights/pallas_call | solution.py:876
  163.0 1.0 collective-permute-start.14
  164.1 15.0 %attend_back.1 = (bf16[2048,128]{1,0:T(8,128)(2,1)}, f32[2048,128]{1,0:T(8,128)}, bf16[1024,128]{1,0:T(8,128)(2,1)}, bf16[1024,128]{1,0:T(8,128)(2,1)}, f32[2,12...) custom-call(s32[1]{0:T(128)} %bitcast.z_ref, ...), custom_call_target="tpu_custom_call" | custom-call | flops 17250000896 | tf_op jit(solution)/shard_map/attend_back/pallas_call | solution.py:478
  179.1 1.4 collective-permute-start.16
  180.5 2.7 fusion.5
  183.2 3.0 %collective-permute-start.32 = (bf16[1120,128]{1,0:T(8,128)(2,1)}, bf16[1120,128]{1,0:T(8,128)(2,1)}, u32[]{:S(2)}, u32[]{:S(2)}) collective-permute-start(bf16[1120,128]{1,0:T(8,128)(2,1)} %get-tuple-element.165.refs_4_), channel_id=1, source_target_pairs={{0,24},{4,28},{8,16},{12,20},{16,8},{20,12},{24,0},{28,4},{1,25},{... | collective-permute-start | bytes 860168 | tf_op jit(solution)/shard_map/ppermute | solution.py:1160
  187.6 13.3 %weight_grads.1 = (bf16[4,912,128]{2,1,0:T(8,128)(2,1)}, bf16[4,912,128]{2,1,0:T(8,128)(2,1)}, f32[8,1024]{1,0:T(8,128)}) custom-call(s32[2]{0:T(128)} %pad_add_fusion.2.where_ref, bf16[2048,1024]{1,0:T(8,128)(2,1)} %get-tuple-element.97.normed_ref, bf16[2048,128]{1,0:T(8,128)(2,1)} %get-tuple-element.104.key_ref, f32[2048,128]{1,0:T(8,128)} %get-tuple-element.105.value_ref, ...), custom_call_target="tpu_custom_call" | custom-call | flops 17250000896 | tf_op jit(solution)/shard_map/weight_grads/pallas_call | solution.py:1018
  200.9 6.3 %token_parts.1 = (f32[256,1024]{1,0:T(8,128)}, bf16[256,1024]{1,0:T(8,128)(2,1)}) custom-call(bf16[2,3,256,128]{3,2,1,0:T(8,128)(2,1)} %get-tuple-element.113.own_ref, bf16[2,3,256,128]{3,2,1,0:T(8,128)(2,1)} %collective-permute-done.16.far_ref, bf16[1024,1024]{1,0:T(8,128)(2,1)} %get-tuple-element.82.w_ref.w_own_ref, bf16[8,128,1024]{2,1,0:T(8,128)(2,1)} %after.35.w_far_ref), custom_call_target="tpu_custom_call" | custom-call | flops 6899999744 | tf_op jit(solution)/shard_map/token_parts/pallas_call | solution.py:1111
  207.3 2.6 collective-permute-start.21
  209.9 2.1 add_convert_fusion.1
  212.0 1.1 collective-permute-start.20
  213.0 1.1 collective-permute-start.19
  214.1 0.9 collective-permute-start.17
  215.1 1.3 convert_add_fusion.1
  217.2 1.9 slice.175.refs_1_
  219.7 0.9 copy-done.2
  221.4 2.4 collective-permute-start.28
  225.0 1.9 collective-permute-start.22
  226.9 2.1 fusion.10
  229.1 1.3 collective-permute-done.17.near_ref
  230.4 2.5 collective-permute-start.25
  234.6 3.5 %token_sum.1 = f32[256,1024]{1,0:T(8,128)} custom-call(s32[1]{0:T(128)} %bitcast.z_ref, bf16[1024,1024]{1,0:T(8,128)(2,1)} %tok_ref.5, f32[256,1024]{1,0:T(8,128)} %get-tuple-element.112.mid_ref, f32[1,1024]{1,0:T(1,128)} %bitcast.129, f32[256,1024]{1,0:T(8,128)} %get-tuple-element.115.own_ref, bf16[256,1024]{1,0:T(8,128)(2,1)} %collective-permute-done.17.near_ref), custom_call_target="tpu_custom_call" | custom-call | flops 4600000000 | tf_op jit(solution)/shard_map/token_sum/pallas_call | solution.py:1137
  238.3 2.0 collective-permute-done.25.refs_3_
  240.3 3.1 %collective-permute-done.24.refs_2_ = bf16[912,128]{1,0:T(8,128)(2,1)} collective-permute-done((bf16[912,128]{1,0:T(8,128)(2,1)}, bf16[912,128]{1,0:T(8,128)(2,1)}, u32[]{:S(2)}, u32[]{:S(2)}) %collective-permute-start.24) | collective-permute-done | bytes 233504 | tf_op jit(solution)/shard_map/ppermute | solution.py:1160
  243.6 11.0 %collective-permute-done.22.refs_0_ = bf16[128,2048]{1,0:T(8,128)(2,1)} collective-permute-done((bf16[128,2048]{1,0:T(8,128)(2,1)}, bf16[128,2048]{1,0:T(8,128)(2,1)}, u32[]{:S(2)}, u32[]{:S(2)}) %collective-permute-start.22) | collective-permute-done | bytes 524320 | tf_op jit(solution)/shard_map/ppermute | solution.py:1160
  254.6 1.5 fusion.1
  258.1 1.7 fusion.6
  259.8 1.2 convert_add_fusion
  261.0 0.9 slice_bitcast_fusion
  262.7 1.0 copy.76
  (159 shorter events, 22.9 us)
Async XLA Ops:
  7.2 7.1 %copy-start.26 = (s32[1,2048]{1,0:T(1,128)S(1)}, s32[1,2048]{1,0:T(1,128)}, u32[]{:S(2)}) copy-start(s32[1,2048]{1,0:T(1,128)} %param.23) | copy-start | bytes 24580
  7.2 7.7 %copy-start.31 = (f32[1,112]{1,0:T(1,128)S(1)}, f32[1,112]{1,0:T(1,128)}, u32[]{:S(2)}) copy-start(f32[1,112]{1,0:T(1,128)} %param.37) | copy-start | bytes 1348
  7.2 8.2 %copy-start.32 = (f32[1,112]{1,0:T(1,128)S(1)}, f32[1,112]{1,0:T(1,128)}, u32[]{:S(2)}) copy-start(f32[1,112]{1,0:T(1,128)} %param.38) | copy-start | bytes 1348
  7.2 87.8 %all-gather.5.cloned.1.call-start = ((), (), s32[]{:S(2)}) async-start(), calls=%async_computation.2 | async-start | bytes 4718592 | tf_op jit(solution)/shard_map/all_gather | solution.py:1299
  8.2 25.7 %collective-permute-start = (bf16[560,128]{1,0:T(8,128)(2,1)S(1)}, bf16[560,128]{1,0:T(8,128)(2,1)S(1)}, u32[]{:S(2)}, u32[]{:S(2)}) collective-permute-start(bf16[560,128]{1,0:T(8,128)(2,1)S(1)} %dynamic-slice_bitcast_fusion.2), channel_id=1, source_target_pairs={{0,2},{1,3},{2,0},{3,1},{4,6},{5,7},{6,4},{7,5},{8,10},{9,11},{10,... | collective-permute-start | bytes 430088 | tf_op jit(solution)/shard_map/ppermute | solution.py:1160
  14.3 28.2 %collective-permute-start.9 = (bf16[2,128,1024]{2,1,0:T(8,128)(2,1)}, bf16[2,128,1024]{2,1,0:T(8,128)(2,1)S(1)}, u32[]{:S(2)}, u32[]{:S(2)}) collective-permute-start(bf16[2,128,1024]{2,1,0:T(8,128)(2,1)} %pad_maximum_fusion.1), channel_id=1, source_target_pairs={{0,2},{1,3},{2,0},{3,1},{4,6},{5,7},{6,4},{7,5},{8,10},{9,11},{10,... | collective-permute-start | bytes 1572872 | tf_op jit(solution)/shard_map/ppermute | solution.py:1160
  33.9 0.7 copy-start.13
  42.4 0.8 copy-start.5
  43.3 87.7 %all-gather.7.cloned.1.call-start = ((), (), s32[]{:S(2)}) async-start(), calls=%async_computation.3 | async-start | bytes 2359296 | tf_op jit(solution)/shard_map/all_gather | solution.py:1321
  43.4 7.2 %collective-permute-start.4 = (bf16[560,128]{1,0:T(8,128)(2,1)}, bf16[560,128]{1,0:T(8,128)(2,1)S(1)}, u32[]{:S(2)}, u32[]{:S(2)}) collective-permute-start(bf16[560,128]{1,0:T(8,128)(2,1)} %after.22.refs_0_), channel_id=1, source_target_pairs={{0,24},{4,28},{8,16},{12,20},{16,8},{20,12},{24,0},{28,4},{1,25},{... | collective-permute-start | bytes 430088 | tf_op jit(solution)/shard_map/ppermute | solution.py:1160
  46.2 6.7 %collective-permute-start.3 = (bf16[560,128]{1,0:T(8,128)(2,1)}, bf16[560,128]{1,0:T(8,128)(2,1)}, u32[]{:S(2)}, u32[]{:S(2)}) collective-permute-start(bf16[560,128]{1,0:T(8,128)(2,1)} %after.22.refs_0_), channel_id=1, source_target_pairs={{0,16},{4,20},{8,24},{12,28},{16,0},{20,4},{24,8},{28,12},{1,17},{... | collective-permute-start | bytes 430088 | tf_op jit(solution)/shard_map/ppermute | solution.py:1160
  46.7 6.3 %collective-permute-start.2 = (bf16[560,128]{1,0:T(8,128)(2,1)}, bf16[560,128]{1,0:T(8,128)(2,1)}, u32[]{:S(2)}, u32[]{:S(2)}) collective-permute-start(bf16[560,128]{1,0:T(8,128)(2,1)} %after.22.refs_0_), channel_id=1, source_target_pairs={{0,8},{4,12},{8,0},{12,4},{16,24},{20,28},{24,16},{28,20},{1,9},{5... | collective-permute-start | bytes 430088 | tf_op jit(solution)/shard_map/ppermute | solution.py:1160
  46.9 8.8 %copy-start.16 = (bf16[256,1024]{1,0:T(8,128)(2,1)S(1)}, bf16[256,1024]{1,0:T(8,128)(2,1)}, u32[]{:S(2)}) copy-start(bf16[256,1024]{1,0:T(8,128)(2,1)} %cot_ref.3) | copy-start | bytes 1572868
  46.9 8.2 %collective-permute-start.1 = (bf16[2,256,128]{2,1,0:T(8,128)(2,1)}, bf16[2,256,128]{2,1,0:T(8,128)(2,1)S(1)}, u32[]{:S(2)}, u32[]{:S(2)}) collective-permute-start(bf16[2,256,128]{2,1,0:T(8,128)(2,1)} %get-tuple-element.80), channel_id=1, source_target_pairs={{0,2},{1,3},{2,0},{3,1},{4,6},{5,7},{6,4},{7,5},{8,10},{9,11},{10,... | collective-permute-start | bytes 393224 | tf_op jit(solution)/shard_map/ppermute | solution.py:1160
  50.5 2.5 copy-start.30
  55.1 0.7 copy-start.8
  55.7 3.0 %collective-permute-start.5 = (bf16[4,560,128]{2,1,0:T(8,128)(2,1)}, bf16[4,560,128]{2,1,0:T(8,128)(2,1)}, u32[]{:S(2)}, u32[]{:S(2)}) collective-permute-start(bf16[4,560,128]{2,1,0:T(8,128)(2,1)} %after.23.refs_3_), channel_id=1, source_target_pairs={{0,4},{4,0},{8,12},{12,8},{16,20},{20,16},{24,28},{28,24},{1,5},{5... | collective-permute-start | bytes 1720328 | tf_op jit(solution)/shard_map/ppermute | solution.py:1160
  57.2 30.6 %collective-permute-start.7 = (bf16[256,1024]{1,0:T(8,128)(2,1)}, bf16[256,1024]{1,0:T(8,128)(2,1)S(1)}, u32[]{:S(2)}, u32[]{:S(2)}) collective-permute-start(bf16[256,1024]{1,0:T(8,128)(2,1)} %after.25), channel_id=1, source_target_pairs={{0,1},{1,0},{2,3},{3,2},{4,5},{5,4},{6,7},{7,6},{8,9},{9,8},{10,11... | collective-permute-start | bytes 1572872 | tf_op jit(solution)/shard_map/ppermute | solution.py:1160
  65.2 23.5 %collective-permute-start.8 = (bf16[256,1024]{1,0:T(8,128)(2,1)}, bf16[256,1024]{1,0:T(8,128)(2,1)}, u32[]{:S(2)}, u32[]{:S(2)}) collective-permute-start(bf16[256,1024]{1,0:T(8,128)(2,1)} %get-tuple-element.83), channel_id=1, source_target_pairs={{0,1},{1,0},{2,3},{3,2},{4,5},{5,4},{6,7},{7,6},{8,9},{9,8},{10,11... | collective-permute-start | bytes 1572872 | tf_op jit(solution)/shard_map/ppermute | solution.py:1160
  67.8 20.0 %collective-permute-start.6 = (bf16[128,1024]{1,0:T(8,128)(2,1)}, bf16[128,1024]{1,0:T(8,128)(2,1)S(1)}, u32[]{:S(2)}, u32[]{:S(2)}) collective-permute-start(bf16[128,1024]{1,0:T(8,128)(2,1)} %after.24), channel_id=1, source_target_pairs={{0,2},{1,3},{2,0},{3,1},{4,6},{5,7},{6,4},{7,5},{8,10},{9,11},{10,... | collective-permute-start | bytes 786440 | tf_op jit(solution)/shard_map/ppermute | solution.py:1160
  87.8 0.7 copy-start.4
  87.8 0.9 copy-start.17
  91.3 125.9 %reduce-scatter.2.cloned.1.call-start = ((), (), s32[]{:S(2)}) async-start(), calls=%async_computation.1 | async-start | bytes 9437184 | tf_op jit(solution)/shard_map/reduce_scatter | solution.py:1329
  91.5 15.5 %collective-permute-start.10 = (bf16[256,1024]{1,0:T(8,128)(2,1)}, bf16[256,1024]{1,0:T(8,128)(2,1)S(1)}, u32[]{:S(2)}, u32[]{:S(2)}) collective-permute-start(bf16[256,1024]{1,0:T(8,128)(2,1)} %get-tuple-element.85.up_ref.refs_0_.refs_1_), channel_id=1, source_target_pairs={{0,1},{1,0},{2,3},{3,2},{4,5},{5,4},{6,7},{7,6},{8,9},{9,8},{10,11... | collective-permute-start | bytes 1572872 | tf_op jit(solution)/shard_map/ppermute | solution.py:1160
  107.0 0.8 copy-start.28
  118.0 13.3 %collective-permute-start.11 = (bf16[256,1024]{1,0:T(8,128)(2,1)}, bf16[256,1024]{1,0:T(8,128)(2,1)S(1)}, u32[]{:S(2)}, u32[]{:S(2)}) collective-permute-start(bf16[256,1024]{1,0:T(8,128)(2,1)} %get-tuple-element.93), channel_id=1, source_target_pairs={{0,1},{1,0},{2,3},{3,2},{4,5},{5,4},{6,7},{7,6},{8,9},{9,8},{10,11... | collective-permute-start | bytes 1572872 | tf_op jit(solution)/shard_map/ppermute | solution.py:1160
  131.2 0.8 copy-start.15
  135.6 12.4 %collective-permute-start.12 = (bf16[256,1024]{1,0:T(8,128)(2,1)}, bf16[256,1024]{1,0:T(8,128)(2,1)S(1)}, u32[]{:S(2)}, u32[]{:S(2)}) collective-permute-start(bf16[256,1024]{1,0:T(8,128)(2,1)} %get-tuple-element.94.own_ref.refs_2_), channel_id=1, source_target_pairs={{0,1},{1,0},{2,3},{3,2},{4,5},{5,4},{6,7},{7,6},{8,9},{9,8},{10,11... | collective-permute-start | bytes 1572872 | tf_op jit(solution)/shard_map/ppermute | solution.py:1160
  148.0 0.8 copy-start.29
  154.9 7.5 %collective-permute-start.13 = (bf16[2,256,128]{2,1,0:T(8,128)(2,1)}, bf16[2,256,128]{2,1,0:T(8,128)(2,1)S(1)}, u32[]{:S(2)}, u32[]{:S(2)}) collective-permute-start(bf16[2,256,128]{2,1,0:T(8,128)(2,1)} %get-tuple-element.96), channel_id=1, source_target_pairs={{0,2},{1,3},{2,0},{3,1},{4,6},{5,7},{6,4},{7,5},{8,10},{9,11},{10,... | collective-permute-start | bytes 393224 | tf_op jit(solution)/shard_map/ppermute | solution.py:1160
  162.1 18.5 %collective-permute-start.15 = (bf16[4,1120,128]{2,1,0:T(8,128)(2,1)}, bf16[4,1120,128]{2,1,0:T(8,128)(2,1)}, u32[]{:S(2)}, u32[]{:S(2)}) collective-permute-start(bf16[4,1120,128]{2,1,0:T(8,128)(2,1)} %get-tuple-element.108), channel_id=1, source_target_pairs={{0,4},{4,0},{8,12},{12,8},{16,20},{20,16},{24,28},{28,24},{1,5},{5... | collective-permute-start | bytes 3440648 | tf_op jit(solution)/shard_map/ppermute | solution.py:1160
  163.0 23.8 %collective-permute-start.14 = (bf16[256,1024]{1,0:T(8,128)(2,1)}, bf16[256,1024]{1,0:T(8,128)(2,1)S(1)}, u32[]{:S(2)}, u32[]{:S(2)}) collective-permute-start(bf16[256,1024]{1,0:T(8,128)(2,1)} %after.31), channel_id=1, source_target_pairs={{0,1},{1,0},{2,3},{3,2},{4,5},{5,4},{6,7},{7,6},{8,9},{9,8},{10,11... | collective-permute-start | bytes 1572872 | tf_op jit(solution)/shard_map/ppermute | solution.py:1160
  179.1 21.9 %collective-permute-start.16 = (bf16[2,3,256,128]{3,2,1,0:T(8,128)(2,1)}, bf16[2,3,256,128]{3,2,1,0:T(8,128)(2,1)}, u32[]{:S(2)}, u32[]{:S(2)}) collective-permute-start(bf16[2,3,256,128]{3,2,1,0:T(8,128)(2,1)} %get-tuple-element.114), channel_id=1, source_target_pairs={{0,2},{1,3},{2,0},{3,1},{4,6},{5,7},{6,4},{7,5},{8,10},{9,11},{10,... | collective-permute-start | bytes 1179656 | tf_op jit(solution)/shard_map/ppermute | solution.py:1160
  183.2 3.6 %copy-start.9 = (bf16[1120,128]{1,0:T(8,128)(2,1)}, bf16[1120,128]{1,0:T(8,128)(2,1)S(1)}, u32[]{:S(2)}) copy-start(bf16[1120,128]{1,0:T(8,128)(2,1)S(1)} %get-tuple-element.167.refs_2_) | copy-start | bytes 860164
  183.2 28.8 %collective-permute-start.32 = (bf16[1120,128]{1,0:T(8,128)(2,1)}, bf16[1120,128]{1,0:T(8,128)(2,1)}, u32[]{:S(2)}, u32[]{:S(2)}) collective-permute-start(bf16[1120,128]{1,0:T(8,128)(2,1)} %get-tuple-element.165.refs_4_), channel_id=1, source_target_pairs={{0,24},{4,28},{8,16},{12,20},{16,8},{20,12},{24,0},{28,4},{1,25},{... | collective-permute-start | bytes 860168 | tf_op jit(solution)/shard_map/ppermute | solution.py:1160
  186.2 26.8 %collective-permute-start.31 = (bf16[1120,128]{1,0:T(8,128)(2,1)}, bf16[1120,128]{1,0:T(8,128)(2,1)}, u32[]{:S(2)}, u32[]{:S(2)}) collective-permute-start(bf16[1120,128]{1,0:T(8,128)(2,1)} %get-tuple-element.166.refs_3_), channel_id=1, source_target_pairs={{0,16},{4,20},{8,24},{12,28},{16,0},{20,4},{24,8},{28,12},{1,17},{... | collective-permute-start | bytes 860168 | tf_op jit(solution)/shard_map/ppermute | solution.py:1160
  186.3 27.8 %collective-permute-start.30 = (bf16[1120,128]{1,0:T(8,128)(2,1)S(1)}, bf16[1120,128]{1,0:T(8,128)(2,1)}, u32[]{:S(2)}, u32[]{:S(2)}) collective-permute-start(bf16[1120,128]{1,0:T(8,128)(2,1)S(1)} %get-tuple-element.167.refs_2_), channel_id=1, source_target_pairs={{0,8},{4,12},{8,0},{12,4},{16,24},{20,28},{24,16},{28,20},{1,9},{5... | collective-permute-start | bytes 860168 | tf_op jit(solution)/shard_map/ppermute | solution.py:1160
  186.8 0.8 copy-start.1
  207.2 11.9 %collective-permute-start.18 = (bf16[4,912,128]{2,1,0:T(8,128)(2,1)}, bf16[4,912,128]{2,1,0:T(8,128)(2,1)S(1)}, u32[]{:S(2)}, u32[]{:S(2)}) collective-permute-start(bf16[4,912,128]{2,1,0:T(8,128)(2,1)} %after.37.refs_1_), channel_id=1, source_target_pairs={{0,4},{4,0},{8,12},{12,8},{16,20},{20,16},{24,28},{28,24},{1,5},{5... | collective-permute-start | bytes 2801672 | tf_op jit(solution)/shard_map/ppermute | solution.py:1160
  207.2 2.6 copy-start.11
  207.2 2.6 copy-start.10
  207.3 11.8 %collective-permute-start.21 = (f32[8,1024]{1,0:T(8,128)}, f32[8,1024]{1,0:T(8,128)S(1)}, u32[]{:S(2)}, u32[]{:S(2)}) collective-permute-start(f32[8,1024]{1,0:T(8,128)} %after.36), channel_id=1, source_target_pairs={{0,3},{1,2},{2,1},{3,0},{4,7},{5,6},{6,5},{7,4},{8,11},{9,10},{10,... | collective-permute-start | bytes 98312 | tf_op jit(solution)/shard_map/ppermute | solution.py:1160
  212.0 2.2 copy-start.27
  212.0 3.1 %copy-start.3 = (bf16[1120,128]{1,0:T(8,128)(2,1)S(1)}, bf16[1120,128]{1,0:T(8,128)(2,1)}, u32[]{:S(2)}) copy-start(bf16[1120,128]{1,0:T(8,128)(2,1)} %get-tuple-element.168.refs_1_) | copy-start | bytes 860164
  212.0 7.1 %collective-permute-start.20 = (f32[8,1024]{1,0:T(8,128)}, f32[8,1024]{1,0:T(8,128)S(1)}, u32[]{:S(2)}, u32[]{:S(2)}) collective-permute-start(f32[8,1024]{1,0:T(8,128)} %after.36), channel_id=1, source_target_pairs={{0,2},{1,3},{2,0},{3,1},{4,6},{5,7},{6,4},{7,5},{8,10},{9,11},{10,... | collective-permute-start | bytes 98312 | tf_op jit(solution)/shard_map/ppermute | solution.py:1160
  213.0 6.0 %collective-permute-start.19 = (f32[8,1024]{1,0:T(8,128)}, f32[8,1024]{1,0:T(8,128)S(1)}, u32[]{:S(2)}, u32[]{:S(2)}) collective-permute-start(f32[8,1024]{1,0:T(8,128)} %after.36), channel_id=1, source_target_pairs={{0,1},{1,0},{2,3},{3,2},{4,5},{5,4},{6,7},{7,6},{8,9},{9,8},{10,11... | collective-permute-start | bytes 98312 | tf_op jit(solution)/shard_map/ppermute | solution.py:1160
  214.1 16.2 %collective-permute-start.17 = (bf16[256,1024]{1,0:T(8,128)(2,1)S(1)}, bf16[256,1024]{1,0:T(8,128)(2,1)}, u32[]{:S(2)}, u32[]{:S(2)}) collective-permute-start(bf16[256,1024]{1,0:T(8,128)(2,1)S(1)} %copy-done.27), channel_id=1, source_target_pairs={{0,1},{1,0},{2,3},{3,2},{4,5},{5,4},{6,7},{7,6},{8,9},{9,8},{10,11... | collective-permute-start | bytes 1572872 | tf_op jit(solution)/shard_map/ppermute | solution.py:1160
  215.1 11.9 %copy-start = (bf16[4,912,128]{2,1,0:T(8,128)(2,1)S(1)}, bf16[4,912,128]{2,1,0:T(8,128)(2,1)}, u32[]{:S(2)}) copy-start(bf16[4,912,128]{2,1,0:T(8,128)(2,1)} %get-tuple-element.111.refs_1_) | copy-start | bytes 2801668
  216.4 12.6 %copy-start.6 = (f32[1120,128]{1,0:T(8,128)}, f32[1120,128]{1,0:T(8,128)S(1)}, u32[]{:S(2)}) copy-start(f32[1120,128]{1,0:T(8,128)S(1)} %convert_add_fusion.1) | copy-start | bytes 1720324
  219.7 0.9 copy-start.2
  221.4 11.4 %collective-permute-start.28 = (f32[8,1024]{1,0:T(8,128)S(1)}, f32[8,1024]{1,0:T(8,128)S(1)}, u32[]{:S(2)}, u32[]{:S(2)}) collective-permute-start(f32[8,1024]{1,0:T(8,128)S(1)} %add_add_fusion.1), channel_id=1, source_target_pairs={{0,24},{4,28},{8,16},{12,20},{16,8},{20,12},{24,0},{28,4},{1,25},{... | collective-permute-start | bytes 98312 | tf_op jit(solution)/shard_map/ppermute | solution.py:1160
  223.9 9.6 %collective-permute-start.27 = (f32[8,1024]{1,0:T(8,128)S(1)}, f32[8,1024]{1,0:T(8,128)S(1)}, u32[]{:S(2)}, u32[]{:S(2)}) collective-permute-start(f32[8,1024]{1,0:T(8,128)S(1)} %add_add_fusion.1), channel_id=1, source_target_pairs={{0,16},{4,20},{8,24},{12,28},{16,0},{20,4},{24,8},{28,12},{1,17},{... | collective-permute-start | bytes 98312 | tf_op jit(solution)/shard_map/ppermute | solution.py:1160
  224.5 13.6 %collective-permute-start.26 = (f32[8,1024]{1,0:T(8,128)S(1)}, f32[8,1024]{1,0:T(8,128)}, u32[]{:S(2)}, u32[]{:S(2)}) collective-permute-start(f32[8,1024]{1,0:T(8,128)S(1)} %add_add_fusion.1), channel_id=1, source_target_pairs={{0,8},{4,12},{8,0},{12,4},{16,24},{20,28},{24,16},{28,20},{1,9},{5... | collective-permute-start | bytes 98312 | tf_op jit(solution)/shard_map/ppermute | solution.py:1160
  225.0 29.6 %collective-permute-start.22 = (bf16[128,2048]{1,0:T(8,128)(2,1)}, bf16[128,2048]{1,0:T(8,128)(2,1)}, u32[]{:S(2)}, u32[]{:S(2)}) collective-permute-start(bf16[128,2048]{1,0:T(8,128)(2,1)} %get-tuple-element.122), channel_id=1, source_target_pairs={{0,2},{1,3},{2,0},{3,1},{4,6},{5,7},{6,4},{7,5},{8,10},{9,11},{10,... | collective-permute-start | bytes 1572872 | tf_op jit(solution)/shard_map/ppermute | solution.py:1160
  230.4 9.9 %collective-permute-start.25 = (bf16[912,128]{1,0:T(8,128)(2,1)}, bf16[912,128]{1,0:T(8,128)(2,1)}, u32[]{:S(2)}, u32[]{:S(2)}) collective-permute-start(bf16[912,128]{1,0:T(8,128)(2,1)} %get-tuple-element.169), channel_id=1, source_target_pairs={{0,24},{4,28},{8,16},{12,20},{16,8},{20,12},{24,0},{28,4},{1,25},{... | collective-permute-start | bytes 700424 | tf_op jit(solution)/shard_map/ppermute | solution.py:1160
  232.9 10.5 %collective-permute-start.24 = (bf16[912,128]{1,0:T(8,128)(2,1)}, bf16[912,128]{1,0:T(8,128)(2,1)}, u32[]{:S(2)}, u32[]{:S(2)}) collective-permute-start(bf16[912,128]{1,0:T(8,128)(2,1)} %get-tuple-element.170), channel_id=1, source_target_pairs={{0,16},{4,20},{8,24},{12,28},{16,0},{20,4},{24,8},{28,12},{1,17},{... | collective-permute-start | bytes 700424 | tf_op jit(solution)/shard_map/ppermute | solution.py:1160
  234.1 9.5 %collective-permute-start.23 = (bf16[912,128]{1,0:T(8,128)(2,1)}, bf16[912,128]{1,0:T(8,128)(2,1)}, u32[]{:S(2)}, u32[]{:S(2)}) collective-permute-start(bf16[912,128]{1,0:T(8,128)(2,1)} %get-tuple-element.171), channel_id=1, source_target_pairs={{0,8},{4,12},{8,0},{12,4},{16,24},{20,28},{24,16},{28,20},{1,9},{5... | collective-permute-start | bytes 700424 | tf_op jit(solution)/shard_map/ppermute | solution.py:1160
  238.1 19.4 %collective-permute-start.33 = (bf16[560,128]{1,0:T(8,128)(2,1)}, bf16[560,128]{1,0:T(8,128)(2,1)S(1)}, u32[]{:S(2)}, u32[]{:S(2)}) collective-permute-start(bf16[560,128]{1,0:T(8,128)(2,1)} %slice.224), channel_id=1, source_target_pairs={{0,2},{1,3},{2,0},{3,1},{4,6},{5,7},{6,4},{7,5},{8,10},{9,11},{10,... | collective-permute-start | bytes 430088 | tf_op jit(solution)/shard_map/ppermute | solution.py:1160
  254.6 3.6 %copy-start.7 = (f32[1120,128]{1,0:T(8,128)S(1)}, f32[1120,128]{1,0:T(8,128)}, u32[]{:S(2)}) copy-start(f32[1120,128]{1,0:T(8,128)} %copy-done.6) | copy-start | bytes 1720324
  256.1 3.7 %copy-start.12 = (bf16[128,4096]{1,0:T(8,128)(2,1)S(1)}, bf16[128,4096]{1,0:T(8,128)(2,1)}, u32[]{:S(2)}) copy-start(bf16[128,4096]{1,0:T(8,128)(2,1)} %reduce-scatter.2.cloned.1.call-done) | copy-start | bytes 3145732
  257.5 0.7 copy-start.14
  259.8 2.1 copy-start.20
  259.8 2.1 copy-start.22
  262.6 2.2 collective-permute-start.29
  (6 other events, 3.7 us)
Sparse Core Ops, SparseCore 0:
  43.4 38.2 all-gather.4
  91.4 28.8 all-gather.6
  132.2 79.8 reduce-scatter.1
